TPU v7x, 128 devices: a whole 4x4x4 slice. The times are simulated.
128 devices in a mesh: ep: 16 (over z, x), dp: 8 (over y, core).
Axes of the slice: x: 4, y: 4, z: 4, core: 2. Of those that a mesh axis runs over, the one named last changes fastest.
Arguments:
- tokens: bfloat16 [8192, 4096], P(('ep', 'dp')), may hold values from -6 to 6
- cotangent: bfloat16 [8192, 4096], P(('ep', 'dp')), may hold values from -6 to 6
- expert_ids: int32 [8192, 8], P(('ep', 'dp')), may hold values from 0 to 15, all different within a row; in each aligned block of 64 rows (0 to 63, 64 to 127, ...) at most 33 rows name the same one
- gate_fixed: int32 [8192, 8], P(('ep', 'dp')), may hold values from 1 to 4095
- gate_up: bfloat16 [16, 4096, 1536], P('ep'), may hold values from -0.09375 to 0.09375
- down_weight: bfloat16 [16, 768, 4096], P('ep'), may hold values from -0.4375 to 0.4375
Outputs:
- layer_out: bfloat16 [8192, 4096], P(('ep', 'dp'))
- token_grad: bfloat16 [8192, 4096], P(('ep', 'dp'))
- gate_up_grad: bfloat16 [16, 4096, 1536], P('ep', 'dp')
- down_grad: bfloat16 [16, 768, 4096], P('ep', None, 'dp')
Inputs may be any that keep to these rules, and one draw needn't show every extreme that they name: `expert_ids`: each row names 8 different experts. Among the tokens of one device (aligned blocks of 64 rows) no expert is named more than 33 times, and in every draw some expert is named exactly 33 times in some block.
All inputs are finite; a program needn't handle non-finite values.
Results may differ from a plain program's by a relative error of at most 0.017.
Values may be sent and summed in bfloat16 or wider, within the bound.
A program may use at most 192 MiB of HBM per device.

v0:
```python
import jax
import jax.numpy as jnp
from jax import lax
from jax.sharding import PartitionSpec as P


def expert_forward(slot_rows, in_matrix, out_matrix):
    hidden_width = out_matrix.shape[0]
    pre_act = jnp.dot(slot_rows, in_matrix, preferred_element_type=jnp.float32)
    gate_pre = pre_act[:, :hidden_width]
    up_pre = pre_act[:, hidden_width:]
    logistic = jax.nn.sigmoid(gate_pre)
    hidden = (gate_pre * logistic * up_pre).astype(jnp.bfloat16)
    expert_out = jnp.dot(hidden, out_matrix, preferred_element_type=jnp.float32).astype(
        jnp.bfloat16
    )
    return (pre_act, hidden, expert_out)


def expert_backward(pre_act, slot_grad, in_matrix, out_matrix):
    hidden_width = out_matrix.shape[0]
    gate_pre = pre_act[:, :hidden_width]
    up_pre = pre_act[:, hidden_width:]
    logistic = jax.nn.sigmoid(gate_pre)
    hidden_grad = lax.dot_general(
        slot_grad, out_matrix, (((1,), (1,)), ((), ())), preferred_element_type=jnp.float32
    )
    pre_grad = jnp.concatenate(
        [
            hidden_grad * up_pre * logistic * (1.0 + gate_pre * (1.0 - logistic)),
            hidden_grad * gate_pre * logistic,
        ],
        axis=1,
    ).astype(jnp.bfloat16)
    slot_input_grad = lax.dot_general(
        pre_grad, in_matrix, (((1,), (1,)), ((), ())), preferred_element_type=jnp.float32
    ).astype(jnp.bfloat16)
    return (pre_grad, slot_input_grad)


def per_device(tokens, cotangent, expert_ids, gate_fixed, gate_up, down_weight):
    tok_rows, model_width = tokens.shape
    top_count = expert_ids.shape[1]
    owners = lax.axis_size("ep")
    capacity = min(tok_rows, tok_rows * top_count * 33 // (32 * owners))
    slot_count = owners * capacity
    pair_count = tok_rows * top_count
    in_matrix = gate_up[0]
    out_matrix = down_weight[0]
    gate_int = gate_fixed.astype(jnp.float32)
    gate_share = gate_int / jnp.sum(gate_int, axis=1, keepdims=True)
    flat_share = gate_share.reshape(pair_count)
    flat_ids = expert_ids.reshape(pair_count)
    onehot = (flat_ids[:, None] == jnp.arange(owners, dtype=jnp.int32)[None, :]).astype(jnp.int32)
    slot_rank = jnp.sum((jnp.cumsum(onehot, axis=0) - onehot) * onehot, axis=1)
    slot_of_pair = flat_ids * capacity + slot_rank
    pair_of_slot = (
        jnp.full((slot_count,), pair_count, jnp.int32)
        .at[slot_of_pair]
        .set(jnp.arange(pair_count, dtype=jnp.int32))
    )
    filled = pair_of_slot < pair_count
    clipped = jnp.minimum(pair_of_slot, pair_count - 1)
    slot_token = clipped // top_count
    slot_gate = jnp.where(filled, flat_share[clipped], 0.0)
    send_rows = jnp.where(filled[:, None], tokens[slot_token], jnp.zeros((), jnp.bfloat16))
    send_rows = send_rows.reshape(owners, capacity, model_width)
    send_grad = (slot_gate[:, None] * cotangent[slot_token].astype(jnp.float32)).astype(
        jnp.bfloat16
    )
    send_grad = send_grad.reshape(owners, capacity, model_width)
    recv_rows = lax.all_to_all(send_rows, "ep", split_axis=0, concat_axis=0, tiled=True).reshape(
        slot_count, model_width
    )
    pre_act, hidden, expert_out = expert_forward(recv_rows, in_matrix, out_matrix)
    back_result = lax.all_to_all(
        expert_out.reshape(owners, capacity, model_width),
        "ep",
        split_axis=0,
        concat_axis=0,
        tiled=True,
    )
    recv_grad = lax.all_to_all(send_grad, "ep", split_axis=0, concat_axis=0, tiled=True).reshape(
        slot_count, model_width
    )
    pre_grad, slot_input_grad = expert_backward(pre_act, recv_grad, in_matrix, out_matrix)
    back_grad = lax.all_to_all(
        slot_input_grad.reshape(owners, capacity, model_width),
        "ep",
        split_axis=0,
        concat_axis=0,
        tiled=True,
    )
    result_rows = back_result.reshape(slot_count, model_width)[slot_of_pair].reshape(
        tok_rows, top_count, model_width
    )
    layer_out = jnp.sum(gate_share[:, :, None] * result_rows.astype(jnp.float32), axis=1).astype(
        jnp.bfloat16
    )
    grad_rows = back_grad.reshape(slot_count, model_width)[slot_of_pair].reshape(
        tok_rows, top_count, model_width
    )
    token_grad = jnp.sum(grad_rows.astype(jnp.float32), axis=1).astype(jnp.bfloat16)
    part_in = lax.dot_general(
        recv_rows, pre_grad, (((0,), (0,)), ((), ())), preferred_element_type=jnp.float32
    )
    part_out = lax.dot_general(
        hidden, recv_grad, (((0,), (0,)), ((), ())), preferred_element_type=jnp.float32
    )
    grad_in, grad_out = (
        lax.psum_scatter(
            part_in.astype(jnp.bfloat16), "dp", scatter_dimension=0, tiled=True
        ).astype(jnp.float32),
        lax.psum_scatter(
            part_out.astype(jnp.bfloat16), "dp", scatter_dimension=1, tiled=True
        ).astype(jnp.float32),
    )
    return (
        layer_out,
        token_grad,
        grad_in.astype(jnp.bfloat16)[None],
        grad_out.astype(jnp.bfloat16)[None],
    )


def solution(mesh):
    placed = (
        P(("ep", "dp"), None),
        P(("ep", "dp"), None),
        P(("ep", "dp"), None),
        P(("ep", "dp"), None),
        P("ep", None, None),
        P("ep", None, None),
    )
    return jax.shard_map(
        per_device,
        mesh=mesh,
        in_specs=placed,
        out_specs=(
            P(("ep", "dp"), None),
            P(("ep", "dp"), None),
            P("ep", "dp", None),
            P("ep", None, "dp"),
        ),
        check_vma=False,
    )
```

profile of v0, /device:TPU:0, one launch (start us, length us, event | category | flops | bytes accessed | tf_op | source)
XLA Modules:
  0.0 433.4 jit_solution(10558963561654537791)
XLA Ops:
  7.2 0.0 copy-start
  7.2 0.7 broadcast_multiply_fusion
  7.9 0.8 copy.13
  8.7 0.1 eq.29
  8.8 0.1 eq.25
  8.9 0.7 convert_reduce_fusion
  9.6 0.7 convert_divide_fusion
  10.3 0.1 copy.11
  10.4 0.0 copy-start.5
  10.4 0.1 reshape.105
  10.5 0.1 copy.12
  10.5 0.1 mul.65
  10.7 1.2 reduce-window.6
  11.8 0.2 slice_reduce_fusion
  12.1 0.1 fusion.17
  12.2 2.4 scatter_custom_fusion
  14.7 4.0 gather_fusion.2
  18.7 0.1 broadcast_in_dim.39
  18.8 0.0 copy-done
  18.8 5.0 %gather_fusion = bf16[528,4096]{1,0:T(8,128)(2,1)} fusion(bf16[64,4096]{1,0:T(8,128)(2,1)S(1)} %copy-done, s32[1024]{0:T(1024)S(1)} %get-tuple-element.12), kind=kCustom, calls=%fused_computation | custom fusion | bytes 8652864 | tf_op jit(solution)/shard_map/gather | solution.py:66
  23.8 0.0 copy-done.5
  23.8 4.6 %gather.18 = bf16[16,33,4096]{2,1,0:T(8,128)(2,1)} reshape(bf16[528,4096]{1,0:T(8,128)(2,1)} %gather_fusion) | data formatting | bytes 8650752 | tf_op jit(solution)/shard_map/gather | solution.py:66
  28.4 5.2 %broadcast_select_fusion = bf16[16,33,4096]{2,1,0:T(8,128)(2,1)} fusion(bf16[16,33,4096]{2,1,0:T(8,128)(2,1)} %gather.18, pred[16,33]{1,0:T(8,128)(4,1)S(1)} %broadcast_in_dim.39), kind=kLoop, calls=%fused_computation.21 | loop fusion | flops 2162688 | bytes 8651280 | tf_op jit(solution)/shard_map/jit(_where)/select_n | solution.py:66
  33.7 0.0 copy-start.2
  33.7 8.1 %all-to-all-start = ((bf16[16,33,4096]{2,1,0:T(8,128)(2,1)}), bf16[16,33,4096]{2,1,0:T(8,128)(2,1)}, u32[]{:S(2)}, u32[]{:S(2)}) async-start(bf16[16,33,4096]{2,1,0:T(8,128)(2,1)} %broadcast_select_fusion), calls=%async_computation | async-start | bytes 10485760 | tf_op jit(solution)/shard_map/all_to_all | solution.py:72
  41.8 0.1 mul.70
  41.9 0.0 copy-done.2
  41.9 5.0 %gather_fusion.3 = bf16[528,4096]{1,0:T(8,128)(2,1)} fusion(bf16[64,4096]{1,0:T(8,128)(2,1)S(1)} %copy-done.2, s32[1024]{0:T(1024)S(1)} %get-tuple-element.12), kind=kCustom, calls=%fused_computation.3 | custom fusion | bytes 8652864 | tf_op jit(solution)/shard_map/gather | solution.py:68
  46.9 9.0 %reshape.111 = f32[16,33,4096]{2,1,0:T(8,128)} reshape(bf16[528,4096]{1,0:T(8,128)(2,1)} %gather_fusion.3) | data formatting | bytes 12976128 | tf_op jit(solution)/shard_map/convert_element_type | solution.py:68
  55.9 7.8 %multiply_convert_fusion = bf16[16,33,4096]{2,1,0:T(8,128)(2,1)} fusion(f32[16,33,4096]{2,1,0:T(8,128)} %reshape.111, f32[16,33]{1,0:T(8,128)S(1)} %mul.70), kind=kLoop, calls=%fused_computation.11 | loop fusion | flops 4325376 | bytes 12978240 | tf_op jit(solution)/shard_map/convert_element_type | solution.py:68
  63.7 56.3 %all-to-all-done = bf16[16,33,4096]{2,1,0:T(8,128)(2,1)} async-done(((bf16[16,33,4096]{2,1,0:T(8,128)(2,1)}), bf16[16,33,4096]{2,1,0:T(8,128)(2,1)}, u32[]{:S(2)}, u32[]{:S(2)}) %all-to-all-start) | async-done | bytes 4325408 | tf_op jit(solution)/shard_map/all_to_all | solution.py:72
  120.0 5.3 %all-to-all-start.2 = ((bf16[16,33,4096]{2,1,0:T(8,128)(2,1)}), bf16[16,33,4096]{2,1,0:T(8,128)(2,1)}, u32[]{:S(2)}, u32[]{:S(2)}) async-start(bf16[16,33,4096]{2,1,0:T(8,128)(2,1)} %multiply_convert_fusion), calls=%async_computation.2 | async-start | bytes 10485760 | tf_op jit(solution)/shard_map/all_to_all | solution.py:83
  125.4 0.2 reduce-scatter.5.cloned.1.call-start
  125.6 4.6 %reshape.102 = bf16[528,4096]{1,0:T(8,128)(2,1)} reshape(bf16[16,33,4096]{2,1,0:T(8,128)(2,1)} %all-to-all-done) | data formatting | bytes 8650752 | tf_op jit(solution)/shard_map/reshape | solution.py:72
  130.2 12.3 %fusion.2 = f32[528,1536]{1,0:T(8,128)} fusion(bf16[528,4096]{1,0:T(8,128)(2,1)} %reshape.102, bf16[1,4096,1536]{2,1,0:T(8,128)(2,1)} %param.10), kind=kOutput, calls=%fused_computation.9 | convolution fusion | flops 6643777536 | bytes 20152320 | tf_op jit(solution)/shard_map/dot_general | solution.py:9
  142.5 58.3 %all-to-all-done.2 = bf16[16,33,4096]{2,1,0:T(8,128)(2,1)} async-done(((bf16[16,33,4096]{2,1,0:T(8,128)(2,1)}), bf16[16,33,4096]{2,1,0:T(8,128)(2,1)}, u32[]{:S(2)}, u32[]{:S(2)}) %all-to-all-start.2) | async-done | bytes 4325408 | tf_op jit(solution)/shard_map/all_to_all | solution.py:83
  200.9 4.7 %reshape.106 = bf16[528,4096]{1,0:T(8,128)(2,1)} reshape(bf16[16,33,4096]{2,1,0:T(8,128)(2,1)} %all-to-all-done.2) | data formatting | bytes 8650752 | tf_op jit(solution)/shard_map/reshape | solution.py:83
  205.5 0.0 copy-start.4
  205.5 9.1 %multiply_convert_fusion.2 = (bf16[528,768]{1,0:T(8,128)(2,1)S(1)}, bf16[528,768]{1,0:T(8,128)(2,1)S(1)}, bf16[528,768]{1,0:T(8,128)(2,1)S(1)}) fusion(f32[528,1536]{1,0:T(8,128)} %fusion.2, bf16[528,4096]{1,0:T(8,128)(2,1)} %reshape.106, bf16[1,768,4096]{2,1,0:T(8,128)(2,1)} %param.11), kind=kOutput, calls=%fused_computation.25 | convolution fusion | flops 3328376832 | bytes 16293888 | tf_op jit(solution)/shard_map/dot_general | solution.py:25
  214.7 0.0 copy-done.4
  214.7 7.0 %convolution_convert_fusion.1 = bf16[768,4096]{1,0:T(8,128)(2,1)} fusion(bf16[528,768]{1,0:T(8,128)(2,1)S(1)} %get-tuple-element.8, bf16[528,4096]{1,0:T(8,128)(2,1)S(1)} %copy-done.4), kind=kOutput, calls=%fused_computation.14 | convolution fusion | flops 3325034496 | bytes 11427840 | tf_op jit(solution)/shard_map/dot_general | solution.py:107
  221.7 0.0 reduce-scatter.5.cloned.1.call-update
  221.8 0.3 reduce-scatter.3.cloned.1.call-start
  222.0 14.9 %convolution_convert_fusion = bf16[4096,1536]{1,0:T(8,128)(2,1)} fusion(bf16[528,4096]{1,0:T(8,128)(2,1)} %reshape.102, bf16[528,768]{1,0:T(8,128)(2,1)S(1)} %get-tuple-element.7, bf16[528,768]{1,0:T(8,128)(2,1)S(1)} %get-tuple-element.6), kind=kOutput, calls=%fused_computation.6 | convolution fusion | flops 6653313024 | bytes 18530304 | tf_op jit(solution)/shard_map/dot_general | solution.py:104
  236.9 0.0 reduce-scatter.3.cloned.1.call-update
  237.0 8.0 %fusion.12 = bf16[528,4096]{1,0:T(8,128)(2,1)} fusion(bf16[528,768]{1,0:T(8,128)(2,1)S(1)} %get-tuple-element.8, bf16[1,768,4096]{2,1,0:T(8,128)(2,1)} %param.11), kind=kOutput, calls=%fused_computation.20 | convolution fusion | flops 3324051456 | bytes 11427840 | tf_op jit(solution)/shard_map/dot_general | solution.py:14
  245.0 4.7 %reshape.103 = bf16[16,33,4096]{2,1,0:T(8,128)(2,1)} reshape(bf16[528,4096]{1,0:T(8,128)(2,1)} %fusion.12) | data formatting | bytes 8650752 | tf_op jit(solution)/shard_map/reshape | solution.py:77
  249.7 5.3 %all-to-all-start.1 = ((bf16[16,33,4096]{2,1,0:T(8,128)(2,1)}), bf16[16,33,4096]{2,1,0:T(8,128)(2,1)}, u32[]{:S(2)}, u32[]{:S(2)}) async-start(bf16[16,33,4096]{2,1,0:T(8,128)(2,1)} %reshape.103), calls=%async_computation.1 | async-start | bytes 10485760 | tf_op jit(solution)/shard_map/all_to_all | solution.py:76
  255.0 18.6 %fusion.9 = bf16[528,4096]{1,0:T(8,128)(2,1)} fusion(bf16[1,4096,1536]{2,1,0:T(8,128)(2,1)} %param.10, bf16[528,768]{1,0:T(8,128)(2,1)S(1)} %get-tuple-element.7, bf16[528,768]{1,0:T(8,128)(2,1)S(1)} %get-tuple-element.6), kind=kOutput, calls=%fused_computation.19 | convolution fusion | flops 6649184256 | bytes 18530304 | tf_op jit(solution)/shard_map/dot_general | solution.py:35
  273.6 4.7 %reshape.107 = bf16[16,33,4096]{2,1,0:T(8,128)(2,1)} reshape(bf16[528,4096]{1,0:T(8,128)(2,1)} %fusion.9) | data formatting | bytes 8650752 | tf_op jit(solution)/shard_map/reshape | solution.py:88
  278.3 48.8 %all-to-all-done.1 = bf16[16,33,4096]{2,1,0:T(8,128)(2,1)} async-done(((bf16[16,33,4096]{2,1,0:T(8,128)(2,1)}), bf16[16,33,4096]{2,1,0:T(8,128)(2,1)}, u32[]{:S(2)}, u32[]{:S(2)}) %all-to-all-start.1) | async-done | bytes 4325408 | tf_op jit(solution)/shard_map/all_to_all | solution.py:76
  327.0 5.2 %all-to-all-start.3 = ((bf16[16,33,4096]{2,1,0:T(8,128)(2,1)}), bf16[16,33,4096]{2,1,0:T(8,128)(2,1)}, u32[]{:S(2)}, u32[]{:S(2)}) async-start(bf16[16,33,4096]{2,1,0:T(8,128)(2,1)} %reshape.107), calls=%async_computation.3 | async-start | bytes 10485760 | tf_op jit(solution)/shard_map/all_to_all | solution.py:87
  332.2 4.7 %reshape.104 = bf16[528,4096]{1,0:T(8,128)(2,1)} reshape(bf16[16,33,4096]{2,1,0:T(8,128)(2,1)} %all-to-all-done.1) | data formatting | bytes 8650752 | tf_op jit(solution)/shard_map/reshape | solution.py:94
  337.0 11.4 %gather_fusion.1 = bf16[512,4096]{1,0:T(8,128)(2,1)} fusion(bf16[528,4096]{1,0:T(8,128)(2,1)} %reshape.104, s32[1024]{0:T(1024)S(1)} %pad_clamp_fusion.1), kind=kCustom, calls=%fused_computation.1 | custom fusion | bytes 8390656 | tf_op jit(solution)/shard_map/gather | solution.py:94
  348.4 51.1 %all-to-all-done.3 = bf16[16,33,4096]{2,1,0:T(8,128)(2,1)} async-done(((bf16[16,33,4096]{2,1,0:T(8,128)(2,1)}), bf16[16,33,4096]{2,1,0:T(8,128)(2,1)}, u32[]{:S(2)}, u32[]{:S(2)}) %all-to-all-start.3) | async-done | bytes 4325408 | tf_op jit(solution)/shard_map/all_to_all | solution.py:87
  399.5 4.6 %reshape.108 = bf16[528,4096]{1,0:T(8,128)(2,1)} reshape(bf16[16,33,4096]{2,1,0:T(8,128)(2,1)} %all-to-all-done.3) | data formatting | bytes 8650752 | tf_op jit(solution)/shard_map/reshape | solution.py:100
  404.1 11.7 %gather_fusion.4 = bf16[512,4096]{1,0:T(8,128)(2,1)} fusion(bf16[528,4096]{1,0:T(8,128)(2,1)} %reshape.108, s32[1024]{0:T(1024)S(1)} %pad_clamp_fusion.1), kind=kCustom, calls=%fused_computation.4 | custom fusion | bytes 8390656 | tf_op jit(solution)/shard_map/gather | solution.py:100
  415.7 0.0 copy-start.3
  415.8 0.0 copy-start.6
  415.8 6.0 %bitcast_reduce_fusion = bf16[64,4096]{1,0:T(8,128)(2,1)} fusion(bf16[512,4096]{1,0:T(8,128)(2,1)} %gather_fusion.4), kind=kLoop, calls=%fused_computation.22 | loop fusion | flops 1835008 | bytes 4718592 | tf_op jit(solution)/shard_map/reduce_sum | solution.py:103
  421.8 0.0 copy-done.3
  421.8 0.0 copy-done.6
  421.8 4.3 fusion.4
  426.0 0.0 copy-done.1
  (12 shorter events, 0.1 us)
Async XLA Ops:
  7.2 11.6 %copy-start = (bf16[64,4096]{1,0:T(8,128)(2,1)S(1)}, bf16[64,4096]{1,0:T(8,128)(2,1)}, u32[]{:S(2)}) copy-start(bf16[64,4096]{1,0:T(8,128)(2,1)} %param.6) | copy-start | bytes 1572868
  10.4 13.4 %copy-start.5 = (f32[64,8]{1,0:T(8,128)}, f32[64,8]{1,0:T(8,128)S(1)}, u32[]{:S(2)}) copy-start(f32[64,8]{1,0:T(8,128)S(1)} %copy.11) | copy-start | bytes 6148
  33.7 8.2 %copy-start.2 = (bf16[64,4096]{1,0:T(8,128)(2,1)S(1)}, bf16[64,4096]{1,0:T(8,128)(2,1)}, u32[]{:S(2)}) copy-start(bf16[64,4096]{1,0:T(8,128)(2,1)} %param.7) | copy-start | bytes 1572868
  33.7 86.3 %all-to-all-start = ((bf16[16,33,4096]{2,1,0:T(8,128)(2,1)}), bf16[16,33,4096]{2,1,0:T(8,128)(2,1)}, u32[]{:S(2)}, u32[]{:S(2)}) async-start(bf16[16,33,4096]{2,1,0:T(8,128)(2,1)} %broadcast_select_fusion), calls=%async_computation | async-start | bytes 10485760 | tf_op jit(solution)/shard_map/all_to_all | solution.py:72
  120.0 80.9 %all-to-all-start.2 = ((bf16[16,33,4096]{2,1,0:T(8,128)(2,1)}), bf16[16,33,4096]{2,1,0:T(8,128)(2,1)}, u32[]{:S(2)}, u32[]{:S(2)}) async-start(bf16[16,33,4096]{2,1,0:T(8,128)(2,1)} %multiply_convert_fusion), calls=%async_computation.2 | async-start | bytes 10485760 | tf_op jit(solution)/shard_map/all_to_all | solution.py:83
  125.4 300.7 %reduce-scatter.5.cloned.1.call-start = ((), (), s32[]{:S(2)}) async-start(), calls=%async_computation.7 | async-start | bytes 7077888 | tf_op jit(solution)/shard_map/reduce_scatter | solution.py:114
  205.5 9.2 %copy-start.4 = (bf16[528,4096]{1,0:T(8,128)(2,1)S(1)}, bf16[528,4096]{1,0:T(8,128)(2,1)}, u32[]{:S(2)}) copy-start(bf16[528,4096]{1,0:T(8,128)(2,1)} %reshape.106) | copy-start | bytes 12976132
  221.8 204.3 %reduce-scatter.3.cloned.1.call-start = ((), (), s32[]{:S(2)}) async-start(), calls=%async_computation.6 | async-start | bytes 14155776 | tf_op jit(solution)/shard_map/reduce_scatter | solution.py:111
  249.7 77.3 %all-to-all-start.1 = ((bf16[16,33,4096]{2,1,0:T(8,128)(2,1)}), bf16[16,33,4096]{2,1,0:T(8,128)(2,1)}, u32[]{:S(2)}, u32[]{:S(2)}) async-start(bf16[16,33,4096]{2,1,0:T(8,128)(2,1)} %reshape.103), calls=%async_computation.1 | async-start | bytes 10485760 | tf_op jit(solution)/shard_map/all_to_all | solution.py:76
  327.0 72.5 %all-to-all-start.3 = ((bf16[16,33,4096]{2,1,0:T(8,128)(2,1)}), bf16[16,33,4096]{2,1,0:T(8,128)(2,1)}, u32[]{:S(2)}, u32[]{:S(2)}) async-start(bf16[16,33,4096]{2,1,0:T(8,128)(2,1)} %reshape.107), calls=%async_computation.3 | async-start | bytes 10485760 | tf_op jit(solution)/shard_map/all_to_all | solution.py:87
  404.1 22.0 %copy-start.1 = (bf16[64,4096]{1,0:T(8,128)(2,1)S(1)}, bf16[64,4096]{1,0:T(8,128)(2,1)}, u32[]{:S(2)}) copy-start(bf16[64,4096]{1,0:T(8,128)(2,1)} %param.6) | copy-start | bytes 1572868
  415.7 6.0 %copy-start.3 = (bf16[512,4096]{1,0:T(8,128)(2,1)S(1)}, bf16[512,4096]{1,0:T(8,128)(2,1)}, u32[]{:S(2)}) copy-start(bf16[512,4096]{1,0:T(8,128)(2,1)} %gather_fusion.1) | copy-start | bytes 12582916
  415.8 6.0 %copy-start.6 = (f32[64,8]{1,0:T(8,128)S(1)}, f32[64,8]{1,0:T(8,128)}, u32[]{:S(2)}) copy-start(f32[64,8]{1,0:T(8,128)} %copy-done.5) | copy-start | bytes 6148
Sparse Core Ops, SparseCore 0:
  221.9 42.2 reduce-scatter.4
  267.1 72.3 reduce-scatter.2
where the time goes:
time: 441 us; the launch traced here: 433 us
  waiting for transfers between devices  215 us (49%)
  local copies, waits for them, and re-layouts  82.9 us (19%)
  matrix products  70 us (16%)
  other arithmetic  26.8 us (6%)
  starting transfers between devices  24.4 us (6%)
  between operations  14.7 us (3%)
    all_to_all x1, waiting for transfers between devices, per_device(): lax.all_to_all(send_grad, 'ep', split_axis=0, concat_axis=0, tiled=True)  58.3 us
    all_to_all x1, waiting for transfers between devices, per_device(): lax.all_to_all(send_rows, 'ep', split_axis=0, concat_axis=0, tiled=True)  56.3 us
    all_to_all x1, waiting for transfers between devices, per_device(): lax.all_to_all(slot_input_grad.reshape(owners, capacity, model_width), 'e...  51.1 us
    all_to_all x1, waiting for transfers between devices, per_device(): lax.all_to_all(expert_out.reshape(owners, capacity, model_width), 'ep', s...  48.8 us
    dot_general x1, matrix products, expert_backward(): lax.dot_general(pre_grad, in_matrix, (((1,), (1,)), ((), ())), preferred_...  18.6 us
    dot_general x1, matrix products, per_device(): lax.dot_general(recv_rows, pre_grad, (((0,), (0,)), ((), ())), preferred_...  14.9 us
    dot_general x1, matrix products, expert_forward(): pre_act = jnp.dot(slot_rows, in_matrix, preferred_element_type=jnp.float32)  12.3 us
    gather x1, local copies, waits for them, and re-layouts, per_device(): back_grad.reshape(slot_count, model_width)[slot_of_pair]  11.7 us
  transfers between devices with their start and end apart: 6, of which 4 were waited for; matrix products, arithmetic and copies ran while one was open for 31% of the time, Pallas kernels for 0%

commit v1 on v0

v1 whole, which is shorter than its diff:
```python
import functools

import jax
import jax.numpy as jnp
from jax import lax
from jax.experimental import pallas as pl
from jax.experimental.pallas import tpu as pltpu
from jax.sharding import PartitionSpec as P

BF16 = jnp.bfloat16
F32 = jnp.float32
MESH = pl.DeviceIdType.MESH
TOK = 64
WIDTH = 4096
HALF = WIDTH // 2
CHUNK = HALF // 4
HID = 768
MAIN = 32
ROWS = 16 * MAIN + 16
ORDER = (2, 1, 3)


def place():
    ep = lax.axis_index("ep")
    return ep // 4, ep % 4


def peer(axis, distance):
    z, x = place()
    if axis == "z":
        z = lax.rem(z + distance, 4)
    else:
        x = lax.rem(x + distance, 4)
    return {"ep": z * 4 + x, "dp": lax.axis_index("dp")}


def first_axis(route):
    return ("z", "x")[route]


def second_axis(route):
    return ("x", "z")[route]


def coord(axis):
    z, x = place()
    return z if axis == "z" else x


def expert_at(route, position):
    z, x = place()
    return z * 4 + position if route == 0 else position * 4 + x


def iota(shape, dim):
    return lax.broadcasted_iota(jnp.int32, shape, dim)


def enter(peers):
    barrier = pltpu.get_barrier_semaphore()
    for device in peers:
        pl.semaphore_signal(barrier, 1, device_id=device, device_id_type=MESH)
    pl.semaphore_wait(barrier, len(peers))


def remote(src, dst, send_sem, recv_sem, device):
    return pltpu.make_async_remote_copy(
        src_ref=src,
        dst_ref=dst,
        send_sem=send_sem,
        recv_sem=recv_sem,
        device_id=device,
        device_id_type=MESH,
    )


def pick_row(table, index):
    rows = iota(table.shape, 0)
    return jnp.sum(jnp.where(rows == index, table, 0.0), axis=0, keepdims=True)


def slot_rows(rank, chunk):
    source = iota((1, 4 * TOK), 1) // TOK
    rank = rank.astype(jnp.int32)
    main = jnp.where(rank >= 0, rank + MAIN * source, -1)
    return jnp.where(rank == MAIN, 4 * MAIN + 4 * chunk + source, main)


def overflow_target(route, shape, dim):
    row = iota(shape, dim)
    sender, chunk, source = row // 16, lax.rem(row, 16) // 4, lax.rem(row, 4)
    slot = sender * 4 + source if route == 0 else source * 4 + sender
    return slot, chunk


def dispatch_kernel(
    ids_ref,
    gate_ref,
    tok_ref,
    cot_ref,
    wgu_hbm,
    wd_hbm,
    out_hbm,
    sig_hbm,
    x_hbm,
    g_hbm,
    h_hbm,
    pg_hbm,
    rank_out,
    share_out,
    wgu,
    wd,
    meta_own,
    meta,
    gathered,
    staged,
    staged_over,
    over,
    xbuf,
    gbuf,
    pre,
    hid,
    pgb,
    obuf,
    sbuf,
    local_sem,
    meta_send,
    meta_recv,
    gat_send,
    gat_recv,
    main_send,
    main_recv,
    over_send,
    over_recv,
):
    z, x = place()
    load_gu = pltpu.make_async_copy(wgu_hbm.at[0], wgu, local_sem.at[0])
    load_d = pltpu.make_async_copy(wd_hbm.at[0], wd, local_sem.at[1])
    load_gu.start()
    load_d.start()

    gates = gate_ref[...].astype(F32)
    share = gates / jnp.sum(gates, axis=0, keepdims=True)
    ids = ids_ref[...]
    expert = iota((16, TOK), 0)
    named = jnp.zeros((16, TOK), F32)
    weight = jnp.zeros((16, TOK), F32)
    for k in range(8):
        hit = ids[k : k + 1, :] == expert
        named += jnp.where(hit, 1.0, 0.0)
        weight += jnp.where(hit, share[k : k + 1, :], 0.0)
    before = jnp.where(iota((TOK, TOK), 0) < iota((TOK, TOK), 1), 1.0, 0.0)
    rank = jnp.dot(named.astype(BF16), before.astype(BF16), preferred_element_type=F32)
    rank = jnp.where(named > 0.0, rank, -1.0)
    meta_own[...] = jnp.concatenate([rank, weight], axis=1)

    enter([peer(axis, d) for axis in ("z", "x") for d in ORDER])

    sends = []
    meta_recvs = []
    for route in range(2):
        here = coord(first_axis(route))
        for d in ORDER:
            copy = remote(
                meta_own,
                meta.at[route, here],
                meta_send.at[route, d],
                meta_recv.at[route, d],
                peer(first_axis(route), d),
            )
            copy.start()
            sends.append(copy)
            meta_recvs.append(copy)
        meta[route, pl.ds(here, 1)] = meta_own[...][None]

    sources = (tok_ref, cot_ref)

    def gather_start(which):
        copies = ([], [])
        for d in ORDER:
            for route in range(2):
                here = coord(first_axis(route))
                copy = remote(
                    sources[which].at[:, pl.ds(route * HALF, HALF)],
                    gathered.at[which, route, pl.ds(pl.multiple_of(here * TOK, TOK), TOK), :],
                    gat_send.at[which, route, d],
                    gat_recv.at[which, route, d],
                    peer(first_axis(route), d),
                )
                copy.start()
                sends.append(copy)
                copies[route].append(copy)
        for route in range(2):
            here = coord(first_axis(route))
            gathered[which, route, pl.ds(pl.multiple_of(here * TOK, TOK), TOK), :] = sources[
                which
            ][:, route * HALF : (route + 1) * HALF]
        return copies

    tok_copies = gather_start(0)
    for copy in meta_recvs:
        copy.wait_recv()
    for route in range(2):
        rank_out[route] = jnp.concatenate([meta[route, s][:, :TOK] for s in range(4)], axis=1)
        share_out[route] = jnp.concatenate([meta[route, s][:, TOK:] for s in range(4)], axis=1)

    buffers = (xbuf, gbuf)

    def select(which, route, d):
        position = lax.rem(coord(second_axis(route)) + d, 4)
        expert = expert_at(route, position)
        rank_row = pick_row(rank_out[route], expert)
        share_row = pick_row(share_out[route], expert)
        here = coord(second_axis(route))
        target = buffers[which]
        total = jnp.zeros((16, CHUNK), F32)
        for c in range(4):
            hit = slot_rows(rank_row, c) == iota((4 * MAIN + 16, 4 * TOK), 0)
            choose = jnp.where(hit, 1.0, 0.0).astype(BF16)
            rows = jnp.dot(
                choose,
                gathered[which, route, :, c * CHUNK : (c + 1) * CHUNK],
                preferred_element_type=F32,
            )
            if which == 1:
                rows = rows * jnp.sum(jnp.where(hit, share_row, 0.0), axis=1, keepdims=True)
            main = rows[: 4 * MAIN].astype(BF16)
            total += rows[4 * MAIN :]
            if d:
                staged[which, route, d - 1, :, c * CHUNK : (c + 1) * CHUNK] = main
            else:
                columns = slice(route * HALF + c * CHUNK, route * HALF + (c + 1) * CHUNK)
                if route == 0:
                    target[pl.ds(pl.multiple_of(here * 128, 128), 128), columns] = main
                else:
                    for s in range(4):
                        first = pl.multiple_of((s * 4 + here) * MAIN, MAIN)
                        target[pl.ds(first, MAIN), columns] = main[s * MAIN : (s + 1) * MAIN]
        mine = pl.ds(pl.multiple_of(here * 16, 16), 16)
        if not d:
            over[which, route, mine, :] = total.astype(BF16)
            return []
        staged_over[which, route, d - 1] = total.astype(BF16)
        device = peer(second_axis(route), d)
        columns = pl.ds(route * HALF, HALF)
        copies = []
        if route == 0:
            copies.append(
                remote(
                    staged.at[which, route, d - 1],
                    target.at[pl.ds(pl.multiple_of(here * 128, 128), 128), columns],
                    main_send.at[which, route, d, 0],
                    main_recv.at[which, route, d, 0],
                    device,
                )
            )
        else:
            for s in range(4):
                first = pl.multiple_of((s * 4 + here) * MAIN, MAIN)
                copies.append(
                    remote(
                        staged.at[which, route, d - 1, pl.ds(s * MAIN, MAIN), :],
                        target.at[pl.ds(first, MAIN), columns],
                        main_send.at[which, route, d, s],
                        main_recv.at[which, route, d, s],
                        device,
                    )
                )
        copies.append(
            remote(
                staged_over.at[which, route, d - 1],
                over.at[which, route, mine, :],
                over_send.at[which, route, d],
                over_recv.at[which, route, d],
                device,
            )
        )
        for copy in copies:
            copy.start()
        sends.extend(copies)
        return copies

    def second_hop(which, gather_copies):
        arrivals = []
        for route in range(2):
            for copy in gather_copies[route]:
                copy.wait_recv()
        for d in ORDER:
            for route in range(2):
                arrivals.extend(select(which, route, d))
        return arrivals

    def finish(which, arrivals):
        for route in range(2):
            select(which, route, 0)
        for copy in arrivals:
            copy.wait_recv()
        for route in range(2):
            slot, chunk = overflow_target(route, (16, 64), 1)
            for c in range(4):
                spread = jnp.where((slot == iota((16, 64), 0)) & (chunk == c), 1.0, 0.0)
                first = route * HALF + c * CHUNK
                buffers[which][16 * MAIN : ROWS, first : first + CHUNK] = jnp.dot(
                    spread.astype(BF16), over[which, route], preferred_element_type=F32
                ).astype(BF16)

    x_arrivals = second_hop(0, tok_copies)
    cot_copies = gather_start(1)
    load_gu.wait()
    load_d.wait()
    g_arrivals = second_hop(1, cot_copies)
    finish(0, x_arrivals)
    store_x = pltpu.make_async_copy(xbuf, x_hbm, local_sem.at[2])
    store_x.start()

    @pl.loop(0, 3)
    def _(n):
        u_cols = pl.ds(pl.multiple_of(n * 256, 256), 256)
        v_cols = pl.ds(pl.multiple_of(HID + n * 256, 256), 256)
        u = jnp.dot(xbuf[...], wgu[:, u_cols], preferred_element_type=F32)
        pre[:, u_cols] = u
        v = jnp.dot(xbuf[...], wgu[:, v_cols], preferred_element_type=F32)
        pre[:, v_cols] = v
        hid[:, u_cols] = (pre[:, u_cols] * jax.nn.sigmoid(pre[:, u_cols]) * v).astype(BF16)

    store_h = pltpu.make_async_copy(hid, h_hbm, local_sem.at[3])
    store_h.start()

    @pl.loop(0, WIDTH // 256)
    def _(n):
        cols = pl.ds(pl.multiple_of(n * 256, 256), 256)
        obuf[:, cols] = jnp.dot(hid[...], wd[:, cols], preferred_element_type=F32).astype(BF16)

    store_o = pltpu.make_async_copy(obuf, out_hbm, local_sem.at[4])
    store_o.start()
    finish(1, g_arrivals)
    store_g = pltpu.make_async_copy(gbuf, g_hbm, local_sem.at[5])
    store_g.start()

    @pl.loop(0, 3)
    def _(n):
        u_cols = pl.ds(pl.multiple_of(n * 256, 256), 256)
        v_cols = pl.ds(pl.multiple_of(HID + n * 256, 256), 256)
        grad = lax.dot_general(
            gbuf[...], wd[u_cols, :], (((1,), (1,)), ((), ())), preferred_element_type=F32
        )
        u = pre[:, u_cols]
        logistic = jax.nn.sigmoid(u)
        pgb[:, v_cols] = (grad * u * logistic).astype(BF16)
        pgb[:, u_cols] = (
            grad * pre[:, v_cols] * logistic * (1.0 + u * (1.0 - logistic))
        ).astype(BF16)

    store_p = pltpu.make_async_copy(pgb, pg_hbm, local_sem.at[6])
    store_p.start()

    @pl.loop(0, WIDTH // 256)
    def _(n):
        cols = pl.ds(pl.multiple_of(n * 256, 256), 256)
        sbuf[:, cols] = lax.dot_general(
            pgb[...], wgu[cols, :], (((1,), (1,)), ((), ())), preferred_element_type=F32
        ).astype(BF16)

    store_s = pltpu.make_async_copy(sbuf, sig_hbm, local_sem.at[7])
    store_s.start()
    for copy in (store_x, store_h, store_o, store_g, store_p, store_s):
        copy.wait()
    for copy in sends:
        copy.wait_send()


def return_kernel(
    out_hbm,
    sig_hbm,
    rank_ref,
    share_ref,
    layer_out,
    token_grad,
    tail,
    compact,
    rows,
    rows_over,
    partial,
    final,
    local_sem,
    main_send,
    main_recv,
    over_send,
    over_recv,
    part_send,
    part_recv,
):
    z, x = place()
    inputs = (out_hbm, sig_hbm)
    loads = []
    for which in range(2):
        copy = pltpu.make_async_copy(
            inputs[which].at[pl.ds(16 * MAIN, 16), :], tail.at[which], local_sem.at[which]
        )
        copy.start()
        loads.append(copy)
    enter([peer(axis, d) for axis in ("z", "x") for d in ORDER])
    sends = []

    def pieces(which, route, position, slot):
        columns = pl.ds(route * HALF, HALF)
        if route == 0:
            first = pl.multiple_of(position * 128, 128)
            return [
                (inputs[which].at[pl.ds(first, 128), columns], rows.at[which, route, slot])
            ]
        found = []
        for s in range(4):
            first = pl.multiple_of((s * 4 + position) * MAIN, MAIN)
            found.append(
                (
                    inputs[which].at[pl.ds(first, MAIN), columns],
                    rows.at[which, route, slot, pl.ds(s * MAIN, MAIN), :],
                )
            )
        return found

    def first_hop(which):
        arrivals = [[], []]
        for d in ORDER:
            for route in range(2):
                here = coord(second_axis(route))
                there = lax.rem(here + d, 4)
                for s, (src, dst) in enumerate(pieces(which, route, there, here)):
                    copy = remote(
                        src,
                        dst,
                        main_send.at[which, route, d, s],
                        main_recv.at[which, route, d, s],
                        peer(second_axis(route), d),
                    )
                    copy.start()
                    sends.append(copy)
                    arrivals[route].append(copy)
        owns = [[], []]
        for route in range(2):
            here = coord(second_axis(route))
            for s, (src, dst) in enumerate(pieces(which, route, here, here)):
                copy = pltpu.make_async_copy(src, dst, local_sem.at[2 + which * 8 + route * 4 + s])
                copy.start()
                owns[route].append(copy)
        loads[which].wait()
        for route in range(2):
            here = coord(second_axis(route))
            slot, chunk = overflow_target(route, (64, 16), 0)
            total = jnp.zeros((64, CHUNK), F32)
            for c in range(4):
                take = jnp.where((slot == iota((64, 16), 1)) & (chunk == c), 1.0, 0.0)
                first = route * HALF + c * CHUNK
                total += jnp.dot(
                    take.astype(BF16),
                    tail[which, :, first : first + CHUNK],
                    preferred_element_type=F32,
                )
            compact[which, route] = total.astype(BF16)
            mine = pl.ds(pl.multiple_of(here * 16, 16), 16)
            rows_over[which, route, mine, :] = compact[which, route, mine, :]
            for d in ORDER:
                there = lax.rem(here + d, 4)
                copy = remote(
                    compact.at[which, route, pl.ds(pl.multiple_of(there * 16, 16), 16), :],
                    rows_over.at[which, route, mine, :],
                    over_send.at[which, route, d],
                    over_recv.at[which, route, d],
                    peer(second_axis(route), d),
                )
                copy.start()
                sends.append(copy)
                arrivals[route].append(copy)
        return arrivals, owns

    def combine(which, arrivals, owns):
        finals = []
        for route in range(2):
            for copy in arrivals[route]:
                copy.wait_recv()
            for copy in owns[route]:
                copy.wait()
            ranks = [pick_row(rank_ref[route], expert_at(route, p)) for p in range(4)]
            shares = [pick_row(share_ref[route], expert_at(route, p)) for p in range(4)]
            for c in range(4):
                main, rest = [], []
                for p in range(4):
                    hit = slot_rows(ranks[p], c) == iota((4 * MAIN + 16, 4 * TOK), 0)
                    value = shares[p] if which == 0 else 1.0
                    spread = jnp.where(hit, value, 0.0)
                    main.append(spread[: 4 * MAIN])
                    rest.append(spread[4 * MAIN :])
                main = jnp.concatenate(main, axis=0).astype(BF16)
                rest = jnp.concatenate(rest, axis=0).astype(BF16)
                columns = slice(c * CHUNK, (c + 1) * CHUNK)
                along = (((0,), (0,)), ((), ()))
                total = lax.dot_general(
                    main,
                    rows[which, route, :, :, columns].reshape(16 * MAIN, CHUNK),
                    along,
                    preferred_element_type=F32,
                ) + lax.dot_general(
                    rest, rows_over[which, route], along, preferred_element_type=F32
                )
                partial[which, route, :, columns] = total.astype(BF16)
            here = coord(first_axis(route))
            for d in ORDER:
                there = lax.rem(here + d, 4)
                copy = remote(
                    partial.at[which, route, pl.ds(pl.multiple_of(there * TOK, TOK), TOK), :],
                    final.at[which, route, d - 1],
                    part_send.at[which, route, d],
                    part_recv.at[which, route, d],
                    peer(first_axis(route), d),
                )
                copy.start()
                sends.append(copy)
                finals.append(copy)
        return finals

    def finish(which, finals, result):
        for copy in finals:
            copy.wait_recv()
        for route in range(2):
            here = coord(first_axis(route))
            own = partial[which, route, pl.ds(pl.multiple_of(here * TOK, TOK), TOK), :]
            total = own.astype(F32)
            for d in range(3):
                total += final[which, route, d].astype(F32)
            result[:, route * HALF : (route + 1) * HALF] = total.astype(BF16)

    out_state = first_hop(0)
    sig_state = first_hop(1)
    out_finals = combine(0, *out_state)
    sig_finals = combine(1, *sig_state)
    finish(0, out_finals, layer_out)
    finish(1, sig_finals, token_grad)
    for copy in sends:
        copy.wait_send()


VMEM = pl.BlockSpec(memory_space=pltpu.VMEM)
ANY = pl.BlockSpec(memory_space=pl.ANY)
DMA = pltpu.SemaphoreType.DMA


def dispatch(ids, gates, tokens, cotangent, gate_up, down_weight):
    wide = jax.ShapeDtypeStruct((ROWS, WIDTH), BF16)
    table = jax.ShapeDtypeStruct((2, 16, 4 * TOK), F32)
    return pl.pallas_call(
        dispatch_kernel,
        out_shape=(
            wide,
            wide,
            wide,
            wide,
            jax.ShapeDtypeStruct((ROWS, HID), BF16),
            jax.ShapeDtypeStruct((ROWS, 2 * HID), BF16),
            table,
            table,
        ),
        in_specs=[VMEM] * 4 + [ANY] * 2,
        out_specs=(ANY,) * 6 + (VMEM,) * 2,
        scratch_shapes=[
            pltpu.VMEM((WIDTH, 2 * HID), BF16),
            pltpu.VMEM((HID, WIDTH), BF16),
            pltpu.VMEM((16, 2 * TOK), F32),
            pltpu.VMEM((2, 4, 16, 2 * TOK), F32),
            pltpu.VMEM((2, 2, 4 * TOK, HALF), BF16),
            pltpu.VMEM((2, 2, 3, 4 * MAIN, HALF), BF16),
            pltpu.VMEM((2, 2, 3, 16, CHUNK), BF16),
            pltpu.VMEM((2, 2, 64, CHUNK), BF16),
            pltpu.VMEM((ROWS, WIDTH), BF16),
            pltpu.VMEM((ROWS, WIDTH), BF16),
            pltpu.VMEM((ROWS, 2 * HID), F32),
            pltpu.VMEM((ROWS, HID), BF16),
            pltpu.VMEM((ROWS, 2 * HID), BF16),
            pltpu.VMEM((ROWS, WIDTH), BF16),
            pltpu.VMEM((ROWS, WIDTH), BF16),
            DMA((8,)),
            DMA((2, 4)),
            DMA((2, 4)),
            DMA((2, 2, 4)),
            DMA((2, 2, 4)),
            DMA((2, 2, 4, 4)),
            DMA((2, 2, 4, 4)),
            DMA((2, 2, 4)),
            DMA((2, 2, 4)),
        ],
        compiler_params=pltpu.CompilerParams(
            collective_id=0, has_side_effects=True, vmem_limit_bytes=60 << 20
        ),
        cost_estimate=pl.CostEstimate(
            flops=20 * 10**9, bytes_accessed=40 * 10**6, transcendentals=10**6
        ),
    )(ids, gates, tokens, cotangent, gate_up, down_weight)


def give_back(out_rows, sig_rows, rank, share):
    result = jax.ShapeDtypeStruct((TOK, WIDTH), BF16)
    return pl.pallas_call(
        return_kernel,
        out_shape=(result, result),
        in_specs=[ANY] * 2 + [VMEM] * 2,
        out_specs=(VMEM, VMEM),
        scratch_shapes=[
            pltpu.VMEM((2, 16, WIDTH), BF16),
            pltpu.VMEM((2, 2, 64, CHUNK), BF16),
            pltpu.VMEM((2, 2, 4, 4 * MAIN, HALF), BF16),
            pltpu.VMEM((2, 2, 64, CHUNK), BF16),
            pltpu.VMEM((2, 2, 4 * TOK, HALF), BF16),
            pltpu.VMEM((2, 2, 3, TOK, HALF), BF16),
            DMA((18,)),
            DMA((2, 2, 4, 4)),
            DMA((2, 2, 4, 4)),
            DMA((2, 2, 4)),
            DMA((2, 2, 4)),
            DMA((2, 2, 4)),
            DMA((2, 2, 4)),
        ],
        compiler_params=pltpu.CompilerParams(
            collective_id=1, has_side_effects=True, vmem_limit_bytes=40 << 20
        ),
        cost_estimate=pl.CostEstimate(
            flops=6 * 10**9, bytes_accessed=300 * 10**6, transcendentals=0
        ),
    )(out_rows, sig_rows, rank, share)


def per_device(tokens, cotangent, expert_ids, gate_fixed, gate_up, down_weight):
    out_rows, sig_rows, x_rows, g_rows, hidden, pre_grad, rank, share = dispatch(
        expert_ids.T, gate_fixed.T, tokens, cotangent, gate_up, down_weight
    )
    along = (((0,), (0,)), ((), ()))
    part_out = lax.dot_general(hidden, g_rows, along, preferred_element_type=F32)
    part_in = lax.dot_general(x_rows, pre_grad, along, preferred_element_type=F32)
    grad_out = lax.psum_scatter(part_out.astype(BF16), "dp", scatter_dimension=1, tiled=True)
    grad_in = lax.psum_scatter(part_in.astype(BF16), "dp", scatter_dimension=0, tiled=True)
    layer_out, token_grad = give_back(out_rows, sig_rows, rank, share)
    return layer_out, token_grad, grad_in[None], grad_out[None]


def solution(mesh):
    rows = P(("ep", "dp"), None)
    return jax.shard_map(
        per_device,
        mesh=mesh,
        in_specs=(rows, rows, rows, rows, P("ep", None, None), P("ep", None, None)),
        out_specs=(rows, rows, P("ep", "dp", None), P("ep", None, "dp")),
        check_vma=False,
    )
```

time: 441 us -> 245 us (0.56); the launches traced: 433 us -> 245 us
  waiting for transfers between devices: 215 us -> 19.7 us
  Pallas kernels: 0 us -> 179 us
  local copies, waits for them, and re-layouts: 82.9 us -> 8.15 us
  matrix products: 70 us -> 23.6 us
  other arithmetic: 26.8 us -> 0 us
  starting transfers between devices: 24.4 us -> 0.26 us
    all_to_all x4 -> x0, waiting for transfers between devices: 214 us -> none  [the longest x1 58.3 us: per_device(): lax.all_to_all(send_grad, 'ep', split_axis=0, concat_axis=0, tiled=True)]
    pallas_call x0 -> x2, Pallas kernels: none -> 179 us  [the longest x1 103 us: dispatch(): pl.pallas_call(dispatch_kernel, out_shape=(wide, wide, wide, wide, jax.Sh...]
    dot_general x6 -> x2, matrix products: 70 us -> 23.6 us  [the longest x1 14.8 us: per_device(): lax.dot_general(x_rows, pre_grad, along, preferred_element_type=F32)]
    gather x6 -> x0, local copies, waits for them, and re-layouts: 41.7 us -> none  [the longest x1 11.7 us: per_device(): back_grad.reshape(slot_count, model_width)[slot_of_pair]]
    reshape x7 -> x0, local copies, waits for them, and re-layouts: 28.1 us -> none  [the longest x1 4.74 us: per_device(): back_result.reshape(slot_count, model_width)[slot_of_pair]]
    all_to_all x4 -> x0, starting transfers between devices: 24 us -> none  [the longest x1 8.14 us: per_device(): lax.all_to_all(send_rows, 'ep', split_axis=0, concat_axis=0, tiled=True)]
    reduce_scatter x2, waiting for transfers between devices: 0.01 us -> 19.6 us  [the longest x1 19.6 us: per_device(): lax.psum_scatter(part_in.astype(BF16), 'dp', scatter_dimension=0, tiled=T...]
    reduce_sum x4 -> x0, other arithmetic: 11.1 us -> none  [the longest x1 5.99 us: per_device(): jnp.sum(grad_rows.astype(jnp.float32), axis=1).astype(jnp.bfloat16)]
  transfers between devices with their start and end apart: 6 -> 2, of which waited for: 4 -> 1; matrix products, arithmetic and copies ran while one was open for 31% -> 6% of each run, Pallas kernels for 0% -> 31%
where the time goes in v1:
time: 245 us
  Pallas kernels  179 us (73%)
  matrix products  23.6 us (10%)
  waiting for transfers between devices  19.7 us (8%)
  between operations  14.1 us (6%)
  local copies, waits for them, and re-layouts  8.15 us (3%)
    pallas_call x1, Pallas kernels, dispatch(): pl.pallas_call(dispatch_kernel, out_shape=(wide, wide, wide, wide, jax.Sh...  103 us
    pallas_call x1, Pallas kernels, give_back(): pl.pallas_call(return_kernel, out_shape=(result, result), in_specs=[ANY]...  76 us
    reduce_scatter x1, waiting for transfers between devices, per_device(): lax.psum_scatter(part_in.astype(BF16), 'dp', scatter_dimension=0, tiled=T...  19.6 us
    dot_general x1, matrix products, per_device(): lax.dot_general(x_rows, pre_grad, along, preferred_element_type=F32)  14.8 us
    dot_general x1, matrix products, per_device(): lax.dot_general(hidden, g_rows, along, preferred_element_type=F32)  8.79 us
    unnamed x12, local copies, waits for them, and re-layouts  8.15 us
  transfers between devices with their start and end apart: 2, of which 1 were waited for; matrix products, arithmetic and copies ran while one was open for 6% of the time, Pallas kernels for 31%

profile of v1, /device:TPU:0, one launch (start us, length us, event | category | flops | bytes accessed | tf_op | source)
XLA Modules:
  0.0 244.7 jit_solution(9789593051813927948)
XLA Ops:
  7.2 0.0 reduce-scatter.5.cloned.1.call-start
  7.2 103.0 %shard_map.93 = (bf16[528,4096]{1,0:T(8,128)(2,1)}, bf16[528,4096]{1,0:T(8,128)(2,1)}, bf16[528,4096]{1,0:T(8,128)(2,1)}, bf16[528,4096]{1,0:T(8,128)(2,1)}, bf1...) custom-call(s32[8,64]{1,0:T(8,128)} %bitcast.10, ...), custom_call_target="tpu_custom_call" | custom-call | flops 20000000000 | bytes 40000000 | tf_op jit(solution)/shard_map/pallas_call | solution.py:551
  110.2 8.8 %convolution_convert_fusion.1 = bf16[768,4096]{1,0:T(8,128)(2,1)} fusion(bf16[528,768]{1,0:T(8,128)(2,1)} %get-tuple-element.22, bf16[528,4096]{1,0:T(8,128)(2,1)} %get-tuple-element.23), kind=kOutput, calls=%fused_computation.1 | convolution fusion | flops 3325034496 | bytes 11427840 | tf_op jit(solution)/shard_map/dot_general | solution.py:636
  119.0 0.0 copy-start.4
  119.0 0.0 reduce-scatter.5.cloned.1.call-update
  119.0 0.2 reduce-scatter.3.cloned.1.call-start
  119.2 1.2 copy-done.4
  120.4 14.8 %convolution_convert_fusion = bf16[4096,1536]{1,0:T(8,128)(2,1)} fusion(bf16[528,4096]{1,0:T(8,128)(2,1)} %get-tuple-element.20, bf16[528,1536]{1,0:T(8,128)(2,1)S(1)} %copy-done.4), kind=kOutput, calls=%fused_computation | convolution fusion | flops 6650068992 | bytes 18530304 | tf_op jit(solution)/shard_map/dot_general | solution.py:637
  135.2 0.0 copy-start.2
  135.2 0.0 copy-start.3
  135.2 0.0 reduce-scatter.3.cloned.1.call-update
  135.2 0.7 copy-done.2
  136.0 0.0 copy-done.3
  136.0 0.0 copy-start
  136.0 2.3 copy-done
  138.3 0.0 copy-start.1
  138.3 2.3 copy-done.1
  140.6 76.0 %shard_map.94 = (bf16[64,4096]{1,0:T(8,128)(2,1)S(1)}, bf16[64,4096]{1,0:T(8,128)(2,1)S(1)}) custom-call(bf16[528,4096]{1,0:T(8,128)(2,1)S(1)} %copy-done, bf16[528,4096]{1,0:T(8,128)(2,1)S(1)} %copy-done.1, f32[2,16,256]{2,1,0:T(8,128)S(1)} %copy-done.2, f32[2,16,256]{2,1,0:T(8,128)S(1)} %copy-done.3), custom_call_target="tpu_custom_call" | custom-call | flops 6000000000 | bytes 300000000 | tf_op jit(solution)/shard_map/pallas_call | solution.py:602
  216.6 0.0 reduce-scatter.5.cloned.1.call-done
  216.6 19.6 %reduce-scatter.3.cloned.1.call-done = bf16[512,1536]{1,0:T(8,128)(2,1)} async-done(((bf16[4096,1536]{1,0:T(8,128)(2,1)}), bf16[512,1536]{1,0:T(8,128)(2,1)}) %reduce-scatter.3.cloned.1.call-update) | async-done | bytes 1572880 | tf_op jit(solution)/shard_map/reduce_scatter | solution.py:639
  236.2 0.8 copy.12
  237.0 0.8 copy.13
Async XLA Ops:
  7.2 209.5 %reduce-scatter.5.cloned.1.call-start = ((), (), s32[]{:S(2)}) async-start(), calls=%async_computation.3 | async-start | bytes 7077888 | tf_op jit(solution)/shard_map/reduce_scatter | solution.py:638
  119.0 1.4 copy-start.4
  119.0 117.2 %reduce-scatter.3.cloned.1.call-start = ((), (), s32[]{:S(2)}) async-start(), calls=%async_computation.2 | async-start | bytes 14155776 | tf_op jit(solution)/shard_map/reduce_scatter | solution.py:639
  135.2 0.8 copy-start.2
  135.2 0.8 copy-start.3
  136.0 2.3 copy-start
  138.3 2.3 copy-start.1
Sparse Core Ops, SparseCore 0:
  119.1 41.9 reduce-scatter.4
  164.1 72.1 reduce-scatter.2

commit v2 on v1

--- a/solution.py
+++ b/solution.py
@@ -34,6 +34,16 @@
     return {"ep": z * 4 + x, "dp": lax.axis_index("dp")}
 
 
+def along_y(distance):
+    dp = lax.axis_index("dp")
+    return {"ep": lax.axis_index("ep"), "dp": lax.rem(dp + 2 * distance, 8)}
+
+
+def other_core():
+    dp = lax.axis_index("dp")
+    return {"ep": lax.axis_index("ep"), "dp": dp + 1 - 2 * lax.rem(dp, 2)}
+
+
 def first_axis(route):
     return ("z", "x")[route]
 
@@ -101,7 +111,6 @@
     wgu_hbm,
     wd_hbm,
     out_hbm,
-    sig_hbm,
     x_hbm,
     g_hbm,
     h_hbm,
@@ -122,7 +131,6 @@
     hid,
     pgb,
     obuf,
-    sbuf,
     local_sem,
     meta_send,
     meta_recv,
@@ -132,6 +140,8 @@
     main_recv,
     over_send,
     over_recv,
+    core_send,
+    core_recv,
 ):
     z, x = place()
     load_gu = pltpu.make_async_copy(wgu_hbm.at[0], wgu, local_sem.at[0])
@@ -154,7 +164,7 @@
     rank = jnp.where(named > 0.0, rank, -1.0)
     meta_own[...] = jnp.concatenate([rank, weight], axis=1)
 
-    enter([peer(axis, d) for axis in ("z", "x") for d in ORDER])
+    enter([peer(axis, d) for axis in ("z", "x") for d in ORDER] + [other_core()])
 
     sends = []
     meta_recvs = []
@@ -175,21 +185,25 @@
 
     sources = (tok_ref, cot_ref)
 
+    def block(which, route, position, columns):
+        rows = pl.ds(pl.multiple_of(position * TOK, TOK), TOK)
+        return gathered.at[which, route, rows, columns]
+
     def gather_start(which):
-        copies = ([], [])
-        for d in ORDER:
+        copies = [{}, {}]
+        for d in (1, 3):
             for route in range(2):
                 here = coord(first_axis(route))
                 copy = remote(
                     sources[which].at[:, pl.ds(route * HALF, HALF)],
-                    gathered.at[which, route, pl.ds(pl.multiple_of(here * TOK, TOK), TOK), :],
+                    block(which, route, here, pl.ds(0, HALF)),
                     gat_send.at[which, route, d],
                     gat_recv.at[which, route, d],
                     peer(first_axis(route), d),
                 )
                 copy.start()
                 sends.append(copy)
-                copies[route].append(copy)
+                copies[route][d] = copy
         for route in range(2):
             here = coord(first_axis(route))
             gathered[which, route, pl.ds(pl.multiple_of(here * TOK, TOK), TOK), :] = sources[
@@ -197,7 +211,28 @@
             ][:, route * HALF : (route + 1) * HALF]
         return copies
 
+    def gather_pass(which, copies):
+        passed = []
+        for d in (1, 3):
+            for route in range(2):
+                copies[route][d].wait_recv()
+                axis = first_axis(route)
+                behind = lax.rem(coord(axis) + 4 - d, 4)
+                columns = pl.ds((d // 2) * (HALF // 2), HALF // 2)
+                copy = remote(
+                    block(which, route, behind, columns),
+                    block(which, route, behind, columns),
+                    gat_send.at[which, route, d - 1],
+                    gat_recv.at[which, route, d - 1],
+                    peer(axis, d),
+                )
+                copy.start()
+                sends.append(copy)
+                passed.append(copy)
+        return passed
+
     tok_copies = gather_start(0)
+    cot_copies = gather_start(1)
     for copy in meta_recvs:
         copy.wait_recv()
     for route in range(2):
@@ -280,11 +315,10 @@
         sends.extend(copies)
         return copies
 
-    def second_hop(which, gather_copies):
+    def second_hop(which, passed):
         arrivals = []
-        for route in range(2):
-            for copy in gather_copies[route]:
-                copy.wait_recv()
+        for copy in passed:
+            copy.wait_recv()
         for d in ORDER:
             for route in range(2):
                 arrivals.extend(select(which, route, d))
@@ -304,14 +338,40 @@
                     spread.astype(BF16), over[which, route], preferred_element_type=F32
                 ).astype(BF16)
 
-    x_arrivals = second_hop(0, tok_copies)
-    cot_copies = gather_start(1)
+    tok_passed = gather_pass(0, tok_copies)
+    cot_passed = gather_pass(1, cot_copies)
+    x_arrivals = second_hop(0, tok_passed)
+    g_arrivals = second_hop(1, cot_passed)
     load_gu.wait()
     load_d.wait()
-    g_arrivals = second_hop(1, cot_copies)
+
+    core = lax.rem(lax.axis_index("dp"), 2)
+    stores = []
+    shared = []
+
+    def store(src, dst):
+        copy = pltpu.make_async_copy(src, dst, local_sem.at[2 + len(stores)])
+        copy.start()
+        stores.append(copy)
+
+    def share(src, dst):
+        slot = len(shared)
+        copy = remote(src, dst, core_send.at[slot], core_recv.at[slot], other_core())
+        copy.start()
+        shared.append(copy)
+
+    mine, theirs = pl.ds(0, ROWS), pl.ds(ROWS, ROWS)
+
+    def split(src, dst):
+        for block in range(4):
+            there = pl.ds(block * 512, 512)
+            keep = pl.ds(pl.multiple_of((2 * block + core) * 512, 512), 512)
+            give = pl.ds(pl.multiple_of((2 * block + 1 - core) * 512, 512), 512)
+            share(src.at[:, give], dst.at[theirs, there])
+            store(src.at[:, keep], dst.at[mine, there])
+
     finish(0, x_arrivals)
-    store_x = pltpu.make_async_copy(xbuf, x_hbm, local_sem.at[2])
-    store_x.start()
+    split(xbuf, x_hbm)
 
     @pl.loop(0, 3)
     def _(n):
@@ -323,19 +383,17 @@
         pre[:, v_cols] = v
         hid[:, u_cols] = (pre[:, u_cols] * jax.nn.sigmoid(pre[:, u_cols]) * v).astype(BF16)
 
-    store_h = pltpu.make_async_copy(hid, h_hbm, local_sem.at[3])
-    store_h.start()
+    share(hid, h_hbm.at[theirs])
+    store(hid, h_hbm.at[mine])
 
     @pl.loop(0, WIDTH // 256)
     def _(n):
         cols = pl.ds(pl.multiple_of(n * 256, 256), 256)
         obuf[:, cols] = jnp.dot(hid[...], wd[:, cols], preferred_element_type=F32).astype(BF16)
 
-    store_o = pltpu.make_async_copy(obuf, out_hbm, local_sem.at[4])
-    store_o.start()
+    store(obuf, out_hbm)
     finish(1, g_arrivals)
-    store_g = pltpu.make_async_copy(gbuf, g_hbm, local_sem.at[5])
-    store_g.start()
+    split(gbuf, g_hbm)
 
     @pl.loop(0, 3)
     def _(n):
@@ -351,19 +409,9 @@
             grad * pre[:, v_cols] * logistic * (1.0 + u * (1.0 - logistic))
         ).astype(BF16)
 
-    store_p = pltpu.make_async_copy(pgb, pg_hbm, local_sem.at[6])
-    store_p.start()
-
-    @pl.loop(0, WIDTH // 256)
-    def _(n):
-        cols = pl.ds(pl.multiple_of(n * 256, 256), 256)
-        sbuf[:, cols] = lax.dot_general(
-            pgb[...], wgu[cols, :], (((1,), (1,)), ((), ())), preferred_element_type=F32
-        ).astype(BF16)
-
-    store_s = pltpu.make_async_copy(sbuf, sig_hbm, local_sem.at[7])
-    store_s.start()
-    for copy in (store_x, store_h, store_o, store_g, store_p, store_s):
+    share(pgb, pg_hbm.at[theirs])
+    store(pgb, pg_hbm.at[mine])
+    for copy in stores + shared:
         copy.wait()
     for copy in sends:
         copy.wait_send()
@@ -371,11 +419,29 @@
 
 def return_kernel(
     out_hbm,
-    sig_hbm,
+    wgu_hbm,
+    x_hbm,
+    g_hbm,
+    h_hbm,
+    pg_hbm,
     rank_ref,
     share_ref,
     layer_out,
     token_grad,
+    grad_in,
+    grad_out,
+    xb,
+    gb,
+    hb,
+    pgb,
+    wgu,
+    sig,
+    sum_in,
+    sum_out,
+    near_in,
+    near_out,
+    far_in,
+    far_out,
     tail,
     compact,
     rows,
@@ -383,23 +449,37 @@
     partial,
     final,
     local_sem,
+    wgu_sem,
     main_send,
     main_recv,
     over_send,
     over_recv,
     part_send,
     part_recv,
+    dp_send,
+    dp_recv,
 ):
     z, x = place()
-    inputs = (out_hbm, sig_hbm)
-    loads = []
-    for which in range(2):
-        copy = pltpu.make_async_copy(
-            inputs[which].at[pl.ds(16 * MAIN, 16), :], tail.at[which], local_sem.at[which]
-        )
+    inputs = (out_hbm, sig)
+    fetch = []
+    for slot, (src, dst) in enumerate(((h_hbm, hb), (g_hbm, gb), (x_hbm, xb), (pg_hbm, pgb))):
+        copy = pltpu.make_async_copy(src, dst, local_sem.at[18 + slot])
         copy.start()
-        loads.append(copy)
-    enter([peer(axis, d) for axis in ("z", "x") for d in ORDER])
+        fetch.append(copy)
+    load_tail = pltpu.make_async_copy(
+        out_hbm.at[pl.ds(16 * MAIN, 16), :], tail, local_sem.at[0]
+    )
+    load_tail.start()
+
+    def wgu_tile(n):
+        rows = pl.ds(pl.multiple_of(n * 256, 256), 256)
+        slot = lax.rem(n, 2)
+        return pltpu.make_async_copy(wgu_hbm.at[0, rows, :], wgu.at[slot], wgu_sem.at[slot])
+
+    wgu_tile(0).start()
+    enter(
+        [peer(axis, d) for axis in ("z", "x") for d in ORDER] + [along_y(d) for d in (1, 3)]
+    )
     sends = []
 
     def pieces(which, route, position, slot):
@@ -444,7 +524,9 @@
                 copy = pltpu.make_async_copy(src, dst, local_sem.at[2 + which * 8 + route * 4 + s])
                 copy.start()
                 owns[route].append(copy)
-        loads[which].wait()
+        if which == 0:
+            load_tail.wait()
+        last = tail if which == 0 else sig.at[pl.ds(16 * MAIN, 16), :]
         for route in range(2):
             here = coord(second_axis(route))
             slot, chunk = overflow_target(route, (64, 16), 0)
@@ -454,7 +536,7 @@
                 first = route * HALF + c * CHUNK
                 total += jnp.dot(
                     take.astype(BF16),
-                    tail[which, :, first : first + CHUNK],
+                    last[:, first : first + CHUNK],
                     preferred_element_type=F32,
                 )
             compact[which, route] = total.astype(BF16)
@@ -530,12 +612,125 @@
                 total += final[which, route, d].astype(F32)
             result[:, route * HALF : (route + 1) * HALF] = total.astype(BF16)
 
+    along = (((0,), (0,)), ((), ()))
+    y = lax.axis_index("dp") // 2
+
+    def weight_block(ahead):
+        first = lax.rem(y + ahead, 4) * 512
+        cols = pl.ds(pl.multiple_of(first, 512), 512)
+
+        @pl.loop(0, 3)
+        def _(n):
+            piece = pl.ds(pl.multiple_of(n * 256, 256), 256)
+            sum_out[ahead, piece, :] = lax.dot_general(
+                hb[:, piece], gb[:, cols], along, preferred_element_type=F32
+            ).astype(BF16)
+
+        @pl.loop(0, 2)
+        def _(n):
+            piece = pl.ds(pl.multiple_of(n * 256, 256), 256)
+            part = pl.ds(pl.multiple_of(first + n * 256, 256), 256)
+            sum_in[ahead, piece, :] = lax.dot_general(
+                xb[:, part], pgb[...], along, preferred_element_type=F32
+            ).astype(BF16)
+
+    half_in = (pl.ds(0, 256), pl.ds(256, 256))
+    half_out = (pl.ds(0, HID // 2), pl.ds(HID // 2, HID // 2))
+
+    def pass_half(ahead, half, side, dst_in, dst_out, slot):
+        found = []
+        for kind, (src, dst) in enumerate(
+            (
+                (sum_out.at[ahead, half_out[half], :], dst_out),
+                (sum_in.at[ahead, half_in[half], :], dst_in),
+            )
+        ):
+            copy = remote(
+                src,
+                dst,
+                dp_send.at[slot, side, kind],
+                dp_recv.at[slot, side, kind],
+                along_y((1, 3)[side]),
+            )
+            copy.start()
+            sends.append(copy)
+            found.append(copy)
+        return found
+
     out_state = first_hop(0)
+    for copy in fetch:
+        copy.wait()
+    weight_block(2)
+    near = [
+        pass_half(2, side, side, near_in.at[side], near_out.at[side], 0) for side in range(2)
+    ]
+    ends = []
+    for side, ahead in ((0, 1), (1, 3)):
+        weight_block(ahead)
+        half = 1 - side
+        ends += pass_half(
+            ahead,
+            half,
+            side,
+            far_in.at[side, half_in[half], :],
+            far_out.at[side, half_out[half], :],
+            1,
+        )
+
+    @pl.loop(0, WIDTH // 256)
+    def _(n):
+        @pl.when(n + 1 < WIDTH // 256)
+        def _():
+            wgu_tile(n + 1).start()
+
+        wgu_tile(n).wait()
+        cols = pl.ds(pl.multiple_of(n * 256, 256), 256)
+        sig[:, cols] = lax.dot_general(
+            pgb[:ROWS, :],
+            wgu[lax.rem(n, 2)],
+            (((1,), (1,)), ((), ())),
+            preferred_element_type=F32,
+        ).astype(BF16)
+
     sig_state = first_hop(1)
+    weight_block(0)
+    for side, ahead in ((0, 1), (1, 3)):
+        for copy in near[side]:
+            copy.wait_recv()
+        part = half_in[side]
+        sum_in[ahead, part, :] = (
+            sum_in[ahead, part, :].astype(F32) + near_in[side].astype(F32)
+        ).astype(BF16)
+        part = half_out[side]
+        sum_out[ahead, part, :] = (
+            sum_out[ahead, part, :].astype(F32) + near_out[side].astype(F32)
+        ).astype(BF16)
+        ends += pass_half(
+            ahead,
+            side,
+            side,
+            far_in.at[side, half_in[side], :],
+            far_out.at[side, half_out[side], :],
+            2,
+        )
     out_finals = combine(0, *out_state)
     sig_finals = combine(1, *sig_state)
     finish(0, out_finals, layer_out)
     finish(1, sig_finals, token_grad)
+    for copy in ends:
+        copy.wait_recv()
+
+    @pl.loop(0, 4)
+    def _(n):
+        part = pl.ds(pl.multiple_of(n * 128, 128), 128)
+        total = sum_in[0, part, :].astype(F32)
+        total += far_in[0, part, :].astype(F32) + far_in[1, part, :].astype(F32)
+        grad_in[part, :] = total.astype(BF16)
+        part = pl.ds(pl.multiple_of(n * 192, 192), 192)
+        total = sum_out[0, part, :].astype(F32)
+        total += far_out[0, part, :].astype(F32) + far_out[1, part, :].astype(F32)
+        grad_out[part, :] = total.astype(BF16)
+
     for copy in sends:
         copy.wait_send()
 
@@ -546,22 +741,20 @@
 
 
 def dispatch(ids, gates, tokens, cotangent, gate_up, down_weight):
-    wide = jax.ShapeDtypeStruct((ROWS, WIDTH), BF16)
     table = jax.ShapeDtypeStruct((2, 16, 4 * TOK), F32)
     return pl.pallas_call(
         dispatch_kernel,
         out_shape=(
-            wide,
-            wide,
-            wide,
-            wide,
-            jax.ShapeDtypeStruct((ROWS, HID), BF16),
-            jax.ShapeDtypeStruct((ROWS, 2 * HID), BF16),
+            jax.ShapeDtypeStruct((ROWS, WIDTH), BF16),
+            jax.ShapeDtypeStruct((2 * ROWS, HALF), BF16),
+            jax.ShapeDtypeStruct((2 * ROWS, HALF), BF16),
+            jax.ShapeDtypeStruct((2 * ROWS, HID), BF16),
+            jax.ShapeDtypeStruct((2 * ROWS, 2 * HID), BF16),
             table,
             table,
         ),
         in_specs=[VMEM] * 4 + [ANY] * 2,
-        out_specs=(ANY,) * 6 + (VMEM,) * 2,
+        out_specs=(ANY,) * 5 + (VMEM,) * 2,
         scratch_shapes=[
             pltpu.VMEM((WIDTH, 2 * HID), BF16),
             pltpu.VMEM((HID, WIDTH), BF16),
@@ -577,8 +770,7 @@
             pltpu.VMEM((ROWS, HID), BF16),
             pltpu.VMEM((ROWS, 2 * HID), BF16),
             pltpu.VMEM((ROWS, WIDTH), BF16),
-            pltpu.VMEM((ROWS, WIDTH), BF16),
-            DMA((8,)),
+            DMA((16,)),
             DMA((2, 4)),
             DMA((2, 4)),
             DMA((2, 2, 4)),
@@ -587,6 +779,8 @@
             DMA((2, 2, 4, 4)),
             DMA((2, 2, 4)),
             DMA((2, 2, 4)),
+            DMA((10,)),
+            DMA((10,)),
         ],
         compiler_params=pltpu.CompilerParams(
             collective_id=0, has_side_effects=True, vmem_limit_bytes=60 << 20
@@ -597,47 +791,64 @@
     )(ids, gates, tokens, cotangent, gate_up, down_weight)
 
 
-def give_back(out_rows, sig_rows, rank, share):
+def give_back(out_rows, gate_up, x_rows, g_rows, hidden, pre_grad, rank, share):
     result = jax.ShapeDtypeStruct((TOK, WIDTH), BF16)
     return pl.pallas_call(
         return_kernel,
-        out_shape=(result, result),
-        in_specs=[ANY] * 2 + [VMEM] * 2,
-        out_specs=(VMEM, VMEM),
+        out_shape=(
+            result,
+            result,
+            jax.ShapeDtypeStruct((512, 2 * HID), BF16),
+            jax.ShapeDtypeStruct((HID, 512), BF16),
+        ),
+        in_specs=[ANY] * 6 + [VMEM] * 2,
+        out_specs=(VMEM,) * 4,
         scratch_shapes=[
-            pltpu.VMEM((2, 16, WIDTH), BF16),
+            pltpu.VMEM((2 * ROWS, HALF), BF16),
+            pltpu.VMEM((2 * ROWS, HALF), BF16),
+            pltpu.VMEM((2 * ROWS, HID), BF16),
+            pltpu.VMEM((2 * ROWS, 2 * HID), BF16),
+            pltpu.VMEM((2, 256, 2 * HID), BF16),
+            pltpu.VMEM((ROWS, WIDTH), BF16),
+            pltpu.VMEM((4, 512, 2 * HID), BF16),
+            pltpu.VMEM((4, HID, 512), BF16),
+            pltpu.VMEM((2, 256, 2 * HID), BF16),
+            pltpu.VMEM((2, HID // 2, 512), BF16),
+            pltpu.VMEM((2, 512, 2 * HID), BF16),
+            pltpu.VMEM((2, HID, 512), BF16),
+            pltpu.VMEM((16, WIDTH), BF16),
             pltpu.VMEM((2, 2, 64, CHUNK), BF16),
             pltpu.VMEM((2, 2, 4, 4 * MAIN, HALF), BF16),
             pltpu.VMEM((2, 2, 64, CHUNK), BF16),
             pltpu.VMEM((2, 2, 4 * TOK, HALF), BF16),
             pltpu.VMEM((2, 2, 3, TOK, HALF), BF16),
-            DMA((18,)),
+            DMA((22,)),
+            DMA((2,)),
             DMA((2, 2, 4, 4)),
             DMA((2, 2, 4, 4)),
             DMA((2, 2, 4)),
             DMA((2, 2, 4)),
             DMA((2, 2, 4)),
             DMA((2, 2, 4)),
+            DMA((3, 2, 2)),
+            DMA((3, 2, 2)),
         ],
         compiler_params=pltpu.CompilerParams(
-            collective_id=1, has_side_effects=True, vmem_limit_bytes=40 << 20
+            collective_id=1, has_side_effects=True, vmem_limit_bytes=62 << 20
         ),
         cost_estimate=pl.CostEstimate(
-            flops=6 * 10**9, bytes_accessed=300 * 10**6, transcendentals=0
+            flops=26 * 10**9, bytes_accessed=100 * 10**6, transcendentals=0
         ),
-    )(out_rows, sig_rows, rank, share)
+    )(out_rows, gate_up, x_rows, g_rows, hidden, pre_grad, rank, share)
 
 
 def per_device(tokens, cotangent, expert_ids, gate_fixed, gate_up, down_weight):
-    out_rows, sig_rows, x_rows, g_rows, hidden, pre_grad, rank, share = dispatch(
+    out_rows, x_rows, g_rows, hidden, pre_grad, rank, share = dispatch(
         expert_ids.T, gate_fixed.T, tokens, cotangent, gate_up, down_weight
     )
-    along = (((0,), (0,)), ((), ()))
-    part_out = lax.dot_general(hidden, g_rows, along, preferred_element_type=F32)
-    part_in = lax.dot_general(x_rows, pre_grad, along, preferred_element_type=F32)
-    grad_out = lax.psum_scatter(part_out.astype(BF16), "dp", scatter_dimension=1, tiled=True)
-    grad_in = lax.psum_scatter(part_in.astype(BF16), "dp", scatter_dimension=0, tiled=True)
-    layer_out, token_grad = give_back(out_rows, sig_rows, rank, share)
+    layer_out, token_grad, grad_in, grad_out = give_back(
+        out_rows, gate_up, x_rows, g_rows, hidden, pre_grad, rank, share
+    )
     return layer_out, token_grad, grad_in[None], grad_out[None]
 
 

time: 245 us -> 190 us (0.78)
  matrix products: 23.6 us -> 0 us
  waiting for transfers between devices: 19.7 us -> 0 us
  between operations: 14.1 us -> 0.66 us
    dot_general x2 -> x0, matrix products: 23.6 us -> none  [the longest x1 14.8 us: per_device(): lax.dot_general(x_rows, pre_grad, along, preferred_element_type=F32)]
    reduce_scatter x2 -> x0, waiting for transfers between devices: 19.6 us -> none  [the longest x1 19.6 us: per_device(): lax.psum_scatter(part_in.astype(BF16), 'dp', scatter_dimension=0, tiled=T...]
    unnamed x12 -> x6, local copies, waits for them, and re-layouts: 8.15 us -> 7.34 us
  transfers between devices with their start and end apart: 2 -> 0, of which waited for: 1 -> 0; matrix products, arithmetic and copies ran while one was open for 6% -> 0% of each run, Pallas kernels for 31% -> 0%
where the time goes in v2:
time: 190 us; the launch traced here: 189 us
  Pallas kernels  181 us (95%)
  local copies, waits for them, and re-layouts  7.34 us (4%)
    pallas_call x1, Pallas kernels, give_back(): pl.pallas_call(return_kernel, out_shape=(result, result, jax.ShapeDtypeSt...  95.1 us
    pallas_call x1, Pallas kernels, dispatch(): pl.pallas_call(dispatch_kernel, out_shape=(jax.ShapeDtypeStruct((ROWS, WI...  85.7 us
    unnamed x6, local copies, waits for them, and re-layouts  7.34 us

profile of v2, /device:TPU:0, one launch (start us, length us, event | category | flops | bytes accessed | tf_op | source)
XLA Modules:
  0.0 188.8 jit_solution(2093305882881461138)
XLA Ops:
  0.6 85.7 %shard_map.93 = (bf16[528,4096]{1,0:T(8,128)(2,1)}, bf16[1056,2048]{1,0:T(8,128)(2,1)}, bf16[1056,2048]{1,0:T(8,128)(2,1)}, bf16[1056,768]{1,0:T(8,128)(2,1)}, b...) custom-call(s32[8,64]{1,0:T(8,128)} %bitcast.6, s32[8,64]{1,0:T(8,128)} %bitcast.7, ...), custom_call_target="tpu_custom_call" | custom-call | flops 20000000000 | bytes 40000000 | tf_op jit(solution)/shard_map/pallas_call | solution.py:745
  86.4 95.1 %shard_map.94 = (bf16[64,4096]{1,0:T(8,128)(2,1)}, bf16[64,4096]{1,0:T(8,128)(2,1)}, bf16[512,1536]{1,0:T(8,128)(2,1)}, bf16[768,512]{1,0:T(8,128)(2,1)}) custom-call(bf16[528,4096]{1,0:T(8,128)(2,1)} %get-tuple-element.15.out_hbm, bf16[1,4096,1536]{2,1,0:T(8,128)(2,1)} %wgu_hbm.3, bf16[1056,2048]{1,0:T(8,128)(2,1)} %get-tuple-element.16.x_hbm, ...), custom_call_target="tpu_custom_call" | custom-call | flops 25999998976 | bytes 100000000 | tf_op jit(solution)/shard_map/pallas_call | solution.py:796
  181.5 0.0 copy-start
  181.5 1.9 %copy.14 = bf16[64,4096]{1,0:T(8,128)(2,1)} copy(bf16[64,4096]{1,0:T(8,128)(2,1)} %get-tuple-element.30) | data formatting | bytes 1048576
  183.4 1.9 copy.15
  185.3 2.7 %copy.16 = bf16[1,512,1536]{2,1,0:T(8,128)(2,1)} copy(bf16[1,512,1536]{2,1,0:T(8,128)(2,1)} %bitcast.4) | data formatting | bytes 3145728
  187.9 0.0 copy-done
  187.9 0.9 copy.17
Async XLA Ops:
  181.5 6.5 %copy-start = (bf16[768,512]{1,0:T(8,128)(2,1)S(1)}, bf16[768,512]{1,0:T(8,128)(2,1)}, u32[]{:S(2)}) copy-start(bf16[768,512]{1,0:T(8,128)(2,1)} %get-tuple-element.25) | copy-start | bytes 2359300

commit v3 on v2

--- a/solution.py
+++ b/solution.py
@@ -114,7 +114,7 @@
     x_hbm,
     g_hbm,
     h_hbm,
-    pg_hbm,
+    pre_hbm,
     rank_out,
     share_out,
     wgu,
@@ -126,10 +126,10 @@
     staged_over,
     over,
     xbuf,
-    gbuf,
+    own,
+    own_over,
     pre,
     hid,
-    pgb,
     obuf,
     local_sem,
     meta_send,
@@ -239,7 +239,7 @@
         rank_out[route] = jnp.concatenate([meta[route, s][:, :TOK] for s in range(4)], axis=1)
         share_out[route] = jnp.concatenate([meta[route, s][:, TOK:] for s in range(4)], axis=1)
 
-    buffers = (xbuf, gbuf)
+    buffers = (xbuf, g_hbm)
 
     def select(which, route, d):
         position = lax.rem(coord(second_axis(route)) + d, 4)
@@ -261,7 +261,9 @@
                 rows = rows * jnp.sum(jnp.where(hit, share_row, 0.0), axis=1, keepdims=True)
             main = rows[: 4 * MAIN].astype(BF16)
             total += rows[4 * MAIN :]
-            if d:
+            if which == 1 and not d:
+                own[route, :, c * CHUNK : (c + 1) * CHUNK] = main
+            elif d:
                 staged[which, route, d - 1, :, c * CHUNK : (c + 1) * CHUNK] = main
             else:
                 columns = slice(route * HALF + c * CHUNK, route * HALF + (c + 1) * CHUNK)
@@ -325,8 +327,6 @@
         return arrivals
 
     def finish(which, arrivals):
-        for route in range(2):
-            select(which, route, 0)
         for copy in arrivals:
             copy.wait_recv()
         for route in range(2):
@@ -334,14 +334,21 @@
             for c in range(4):
                 spread = jnp.where((slot == iota((16, 64), 0)) & (chunk == c), 1.0, 0.0)
                 first = route * HALF + c * CHUNK
-                buffers[which][16 * MAIN : ROWS, first : first + CHUNK] = jnp.dot(
+                tail = jnp.dot(
                     spread.astype(BF16), over[which, route], preferred_element_type=F32
                 ).astype(BF16)
+                if which == 0:
+                    xbuf[16 * MAIN : ROWS, first : first + CHUNK] = tail
+                else:
+                    own_over[:, first : first + CHUNK] = tail
 
     tok_passed = gather_pass(0, tok_copies)
     cot_passed = gather_pass(1, cot_copies)
     x_arrivals = second_hop(0, tok_passed)
     g_arrivals = second_hop(1, cot_passed)
+    for which in range(2):
+        for route in range(2):
+            select(which, route, 0)
     load_gu.wait()
     load_d.wait()
 
@@ -359,6 +366,20 @@
         copy = remote(src, dst, core_send.at[slot], core_recv.at[slot], other_core())
         copy.start()
         shared.append(copy)
+
+    for route in range(2):
+        here = coord(second_axis(route))
+        columns = pl.ds(route * HALF, HALF)
+        if route == 0:
+            first = pl.multiple_of(here * 128, 128)
+            store(own.at[route], g_hbm.at[pl.ds(first, 128), columns])
+        else:
+            for s in range(4):
+                first = pl.multiple_of((s * 4 + here) * MAIN, MAIN)
+                store(
+                    own.at[route, pl.ds(s * MAIN, MAIN), :],
+                    g_hbm.at[pl.ds(first, MAIN), columns],
+                )
 
     mine, theirs = pl.ds(0, ROWS), pl.ds(ROWS, ROWS)
 
@@ -384,6 +405,7 @@
         hid[:, u_cols] = (pre[:, u_cols] * jax.nn.sigmoid(pre[:, u_cols]) * v).astype(BF16)
 
     share(hid, h_hbm.at[theirs])
+    store(pre, pre_hbm)
     store(hid, h_hbm.at[mine])
 
     @pl.loop(0, WIDTH // 256)
@@ -393,24 +415,7 @@
 
     store(obuf, out_hbm)
     finish(1, g_arrivals)
-    split(gbuf, g_hbm)
-
-    @pl.loop(0, 3)
-    def _(n):
-        u_cols = pl.ds(pl.multiple_of(n * 256, 256), 256)
-        v_cols = pl.ds(pl.multiple_of(HID + n * 256, 256), 256)
-        grad = lax.dot_general(
-            gbuf[...], wd[u_cols, :], (((1,), (1,)), ((), ())), preferred_element_type=F32
-        )
-        u = pre[:, u_cols]
-        logistic = jax.nn.sigmoid(u)
-        pgb[:, v_cols] = (grad * u * logistic).astype(BF16)
-        pgb[:, u_cols] = (
-            grad * pre[:, v_cols] * logistic * (1.0 + u * (1.0 - logistic))
-        ).astype(BF16)
-
-    share(pgb, pg_hbm.at[theirs])
-    store(pgb, pg_hbm.at[mine])
+    store(own_over, g_hbm.at[pl.ds(16 * MAIN, 16), :])
     for copy in stores + shared:
         copy.wait()
     for copy in sends:
@@ -423,24 +428,27 @@
     x_hbm,
     g_hbm,
     h_hbm,
-    pg_hbm,
+    pre_hbm,
+    wd_hbm,
     rank_ref,
     share_ref,
     layer_out,
     token_grad,
-    grad_in,
     grad_out,
+    own_in,
+    far_in,
     xb,
     gb,
+    gall,
     hb,
+    pre,
+    wd,
     pgb,
     wgu,
-    sig,
     sum_in,
     sum_out,
     near_in,
     near_out,
-    far_in,
     far_out,
     tail,
     compact,
@@ -458,14 +466,36 @@
     part_recv,
     dp_send,
     dp_recv,
+    core_send,
+    core_recv,
 ):
     z, x = place()
+    y = lax.axis_index("dp") // 2
+    core = lax.rem(lax.axis_index("dp"), 2)
+    sig = gall
     inputs = (out_hbm, sig)
-    fetch = []
-    for slot, (src, dst) in enumerate(((h_hbm, hb), (g_hbm, gb), (x_hbm, xb), (pg_hbm, pgb))):
-        copy = pltpu.make_async_copy(src, dst, local_sem.at[18 + slot])
+    mine, theirs = pl.ds(0, ROWS), pl.ds(ROWS, ROWS)
+    fetch = {}
+
+    def load(name, src, dst):
+        copy = pltpu.make_async_copy(src, dst, local_sem.at[18 + len(fetch)])
         copy.start()
-        fetch.append(copy)
+        fetch[name] = copy
+
+    def columns_of(ahead, of_core):
+        first = (2 * lax.rem(y + ahead, 4) + of_core) * 512
+        return pl.ds(pl.multiple_of(first, 512), 512)
+
+    def place_of(ahead):
+        return pl.ds(pl.multiple_of(lax.rem(y + ahead, 4) * 512, 512), 512)
+
+    load("h", h_hbm, hb)
+    for ahead in (2, 1, 3, 0):
+        load(ahead, g_hbm.at[:, columns_of(ahead, core)], gb.at[mine, place_of(ahead)])
+    load("g", g_hbm, gall)
+    load("d", wd_hbm.at[0], wd)
+    load("pre", pre_hbm, pre)
+    load("x", x_hbm, xb)
     load_tail = pltpu.make_async_copy(
         out_hbm.at[pl.ds(16 * MAIN, 16), :], tail, local_sem.at[0]
     )
@@ -478,9 +508,21 @@
 
     wgu_tile(0).start()
     enter(
-        [peer(axis, d) for axis in ("z", "x") for d in ORDER] + [along_y(d) for d in (1, 3)]
+        [peer(axis, d) for axis in ("z", "x") for d in ORDER]
+        + [along_y(d) for d in (1, 3)]
+        + [other_core()]
     )
     sends = []
+    swaps = {}
+    for ahead in (2, 1, 3, 0):
+        swaps[ahead] = remote(
+            g_hbm.at[:, columns_of(ahead, 1 - core)],
+            gb.at[theirs, place_of(ahead)],
+            core_send.at[ahead],
+            core_recv.at[ahead],
+            other_core(),
+        )
+        swaps[ahead].start()
 
     def pieces(which, route, position, slot):
         columns = pl.ds(route * HALF, HALF)
@@ -613,11 +655,9 @@
             result[:, route * HALF : (route + 1) * HALF] = total.astype(BF16)
 
     along = (((0,), (0,)), ((), ()))
-    y = lax.axis_index("dp") // 2
-
-    def weight_block(ahead):
-        first = lax.rem(y + ahead, 4) * 512
-        cols = pl.ds(pl.multiple_of(first, 512), 512)
+
+    def weight_out(ahead):
+        cols = place_of(ahead)
 
         @pl.loop(0, 3)
         def _(n):
@@ -625,6 +665,9 @@
             sum_out[ahead, piece, :] = lax.dot_general(
                 hb[:, piece], gb[:, cols], along, preferred_element_type=F32
             ).astype(BF16)
+
+    def weight_in(ahead):
+        first = lax.rem(y + ahead, 4) * 512
 
         @pl.loop(0, 2)
         def _(n):
@@ -637,45 +680,84 @@
     half_in = (pl.ds(0, 256), pl.ds(256, 256))
     half_out = (pl.ds(0, HID // 2), pl.ds(HID // 2, HID // 2))
 
-    def pass_half(ahead, half, side, dst_in, dst_out, slot):
+    sums = (sum_out, sum_in)
+    nears = (near_out, near_in)
+    fars = (far_out, far_in)
+    halves = (half_out, half_in)
+
+    def pass_half(kind, ahead, half, side, dst, slot):
+        copy = remote(
+            sums[kind].at[ahead, halves[kind][half], :],
+            dst,
+            dp_send.at[slot, side, kind],
+            dp_recv.at[slot, side, kind],
+            along_y((1, 3)[side]),
+        )
+        copy.start()
+        sends.append(copy)
+        return copy
+
+    def pass_near(kind):
+        return [pass_half(kind, 2, side, side, nears[kind].at[side], 0) for side in range(2)]
+
+    def pass_far(kind, side):
+        ahead, half = (1, 3)[side], 1 - side
+        return pass_half(kind, ahead, half, side, fars[kind].at[side, halves[kind][half], :], 1)
+
+    def pass_sum(kind, near):
         found = []
-        for kind, (src, dst) in enumerate(
-            (
-                (sum_out.at[ahead, half_out[half], :], dst_out),
-                (sum_in.at[ahead, half_in[half], :], dst_in),
+        for side, ahead in ((0, 1), (1, 3)):
+            near[side].wait_recv()
+            part = halves[kind][side]
+            sums[kind][ahead, part, :] = (
+                sums[kind][ahead, part, :].astype(F32) + nears[kind][side].astype(F32)
+            ).astype(BF16)
+            found.append(
+                pass_half(kind, ahead, side, side, fars[kind].at[side, part, :], 2)
             )
-        ):
-            copy = remote(
-                src,
-                dst,
-                dp_send.at[slot, side, kind],
-                dp_recv.at[slot, side, kind],
-                along_y((1, 3)[side]),
-            )
-            copy.start()
-            sends.append(copy)
-            found.append(copy)
         return found
 
-    out_state = first_hop(0)
-    for copy in fetch:
-        copy.wait()
-    weight_block(2)
-    near = [
-        pass_half(2, side, side, near_in.at[side], near_out.at[side], 0) for side in range(2)
-    ]
-    ends = []
-    for side, ahead in ((0, 1), (1, 3)):
-        weight_block(ahead)
-        half = 1 - side
-        ends += pass_half(
-            ahead,
-            half,
-            side,
-            far_in.at[side, half_in[half], :],
-            far_out.at[side, half_out[half], :],
-            1,
+    ends_out, ends_in = [], []
+    fetch["h"].wait()
+    for ahead in (2, 1, 3):
+        fetch[ahead].wait()
+        swaps[ahead].wait_recv()
+        weight_out(ahead)
+        if ahead == 2:
+            near_sent_out = pass_near(0)
+            out_state = first_hop(0)
+        else:
+            ends_out.append(pass_far(0, ahead // 2))
+    fetch["g"].wait()
+    fetch["d"].wait()
+    fetch["pre"].wait()
+
+    @pl.loop(0, 3)
+    def _(n):
+        u_cols = pl.ds(pl.multiple_of(n * 256, 256), 256)
+        v_cols = pl.ds(pl.multiple_of(HID + n * 256, 256), 256)
+        grad = lax.dot_general(
+            gall[...], wd[u_cols, :], (((1,), (1,)), ((), ())), preferred_element_type=F32
         )
+        u = pre[:, u_cols]
+        logistic = jax.nn.sigmoid(u)
+        pgb[:ROWS, v_cols] = (grad * u * logistic).astype(BF16)
+        pgb[:ROWS, u_cols] = (
+            grad * pre[:, v_cols] * logistic * (1.0 + u * (1.0 - logistic))
+        ).astype(BF16)
+
+    swap = remote(
+        pgb.at[mine], pgb.at[theirs], core_send.at[4], core_recv.at[4], other_core()
+    )
+    swap.start()
+    fetch["x"].wait()
+    swap.wait_recv()
+    weight_in(2)
+    near_sent_in = pass_near(1)
+    ends_out += pass_sum(0, near_sent_out)
+    for ahead in (1, 3):
+        weight_in(ahead)
+        ends_in.append(pass_far(1, ahead // 2))
 
     @pl.loop(0, WIDTH // 256)
     def _(n):
@@ -693,46 +775,40 @@
         ).astype(BF16)
 
     sig_state = first_hop(1)
-    weight_block(0)
-    for side, ahead in ((0, 1), (1, 3)):
-        for copy in near[side]:
-            copy.wait_recv()
-        part = half_in[side]
-        sum_in[ahead, part, :] = (
-            sum_in[ahead, part, :].astype(F32) + near_in[side].astype(F32)
-        ).astype(BF16)
-        part = half_out[side]
-        sum_out[ahead, part, :] = (
-            sum_out[ahead, part, :].astype(F32) + near_out[side].astype(F32)
-        ).astype(BF16)
-        ends += pass_half(
-            ahead,
-            side,
-            side,
-            far_in.at[side, half_in[side], :],
-            far_out.at[side, half_out[side], :],
-            2,
-        )
+    fetch[0].wait()
+    swaps[0].wait_recv()
+    weight_out(0)
+    weight_in(0)
+    store_own = pltpu.make_async_copy(sum_in.at[0], own_in, local_sem.at[1])
+    store_own.start()
     out_finals = combine(0, *out_state)
-    sig_finals = combine(1, *sig_state)
-    finish(0, out_finals, layer_out)
-    finish(1, sig_finals, token_grad)
-    for copy in ends:
+    ends_in += pass_sum(1, near_sent_in)
+    for copy in ends_out:
         copy.wait_recv()
 
     @pl.loop(0, 4)
     def _(n):
-        part = pl.ds(pl.multiple_of(n * 128, 128), 128)
-        total = sum_in[0, part, :].astype(F32)
-        total += far_in[0, part, :].astype(F32) + far_in[1, part, :].astype(F32)
-        grad_in[part, :] = total.astype(BF16)
         part = pl.ds(pl.multiple_of(n * 192, 192), 192)
         total = sum_out[0, part, :].astype(F32)
         total += far_out[0, part, :].astype(F32) + far_out[1, part, :].astype(F32)
         grad_out[part, :] = total.astype(BF16)
 
-    for copy in sends:
+    finish(0, out_finals, layer_out)
+    sig_finals = combine(1, *sig_state)
+    finish(1, sig_finals, token_grad)
+    store_own.wait()
+    for copy in ends_in:
+        copy.wait_recv()
+    for copy in sends + [swaps[ahead] for ahead in range(4)] + [swap]:
         copy.wait_send()
+
+
+def last_kernel(out_in, grad_in, down_in, own_in, far_in, layer_out, token_grad, gate_up, down):
+    layer_out[...] = out_in[...]
+    token_grad[...] = grad_in[...]
+    down[...] = down_in[...]
+    total = far_in[0].astype(F32) + far_in[1].astype(F32)
+    gate_up[...] = (total + own_in[...].astype(F32)).astype(BF16)
 
 
 VMEM = pl.BlockSpec(memory_space=pltpu.VMEM)
@@ -747,9 +823,9 @@
         out_shape=(
             jax.ShapeDtypeStruct((ROWS, WIDTH), BF16),
             jax.ShapeDtypeStruct((2 * ROWS, HALF), BF16),
-            jax.ShapeDtypeStruct((2 * ROWS, HALF), BF16),
+            jax.ShapeDtypeStruct((ROWS, WIDTH), BF16),
             jax.ShapeDtypeStruct((2 * ROWS, HID), BF16),
-            jax.ShapeDtypeStruct((2 * ROWS, 2 * HID), BF16),
+            jax.ShapeDtypeStruct((ROWS, 2 * HID), F32),
             table,
             table,
         ),
@@ -765,10 +841,10 @@
             pltpu.VMEM((2, 2, 3, 16, CHUNK), BF16),
             pltpu.VMEM((2, 2, 64, CHUNK), BF16),
             pltpu.VMEM((ROWS, WIDTH), BF16),
-            pltpu.VMEM((ROWS, WIDTH), BF16),
+            pltpu.VMEM((2, 4 * MAIN, HALF), BF16),
+            pltpu.VMEM((16, WIDTH), BF16),
             pltpu.VMEM((ROWS, 2 * HID), F32),
             pltpu.VMEM((ROWS, HID), BF16),
-            pltpu.VMEM((ROWS, 2 * HID), BF16),
             pltpu.VMEM((ROWS, WIDTH), BF16),
             DMA((16,)),
             DMA((2, 4)),
@@ -779,8 +855,8 @@
             DMA((2, 2, 4, 4)),
             DMA((2, 2, 4)),
             DMA((2, 2, 4)),
-            DMA((10,)),
-            DMA((10,)),
+            DMA((5,)),
+            DMA((5,)),
         ],
         compiler_params=pltpu.CompilerParams(
             collective_id=0, has_side_effects=True, vmem_limit_bytes=60 << 20
@@ -791,30 +867,32 @@
     )(ids, gates, tokens, cotangent, gate_up, down_weight)
 
 
-def give_back(out_rows, gate_up, x_rows, g_rows, hidden, pre_grad, rank, share):
+def give_back(out_rows, gate_up, x_rows, g_rows, hidden, pre_act, down_weight, rank, share):
     result = jax.ShapeDtypeStruct((TOK, WIDTH), BF16)
     return pl.pallas_call(
         return_kernel,
         out_shape=(
             result,
             result,
+            jax.ShapeDtypeStruct((HID, 512), BF16),
             jax.ShapeDtypeStruct((512, 2 * HID), BF16),
-            jax.ShapeDtypeStruct((HID, 512), BF16),
+            jax.ShapeDtypeStruct((2, 512, 2 * HID), BF16),
         ),
-        in_specs=[ANY] * 6 + [VMEM] * 2,
-        out_specs=(VMEM,) * 4,
+        in_specs=[ANY] * 7 + [VMEM] * 2,
+        out_specs=(VMEM,) * 3 + (ANY,) * 2,
         scratch_shapes=[
             pltpu.VMEM((2 * ROWS, HALF), BF16),
             pltpu.VMEM((2 * ROWS, HALF), BF16),
+            pltpu.VMEM((ROWS, WIDTH), BF16),
             pltpu.VMEM((2 * ROWS, HID), BF16),
+            pltpu.VMEM((ROWS, 2 * HID), F32),
+            pltpu.VMEM((HID, WIDTH), BF16),
             pltpu.VMEM((2 * ROWS, 2 * HID), BF16),
             pltpu.VMEM((2, 256, 2 * HID), BF16),
-            pltpu.VMEM((ROWS, WIDTH), BF16),
             pltpu.VMEM((4, 512, 2 * HID), BF16),
             pltpu.VMEM((4, HID, 512), BF16),
             pltpu.VMEM((2, 256, 2 * HID), BF16),
             pltpu.VMEM((2, HID // 2, 512), BF16),
-            pltpu.VMEM((2, 512, 2 * HID), BF16),
             pltpu.VMEM((2, HID, 512), BF16),
             pltpu.VMEM((16, WIDTH), BF16),
             pltpu.VMEM((2, 2, 64, CHUNK), BF16),
@@ -822,7 +900,7 @@
             pltpu.VMEM((2, 2, 64, CHUNK), BF16),
             pltpu.VMEM((2, 2, 4 * TOK, HALF), BF16),
             pltpu.VMEM((2, 2, 3, TOK, HALF), BF16),
-            DMA((22,)),
+            DMA((27,)),
             DMA((2,)),
             DMA((2, 2, 4, 4)),
             DMA((2, 2, 4, 4)),
@@ -832,6 +910,8 @@
             DMA((2, 2, 4)),
             DMA((3, 2, 2)),
             DMA((3, 2, 2)),
+            DMA((5,)),
+            DMA((5,)),
         ],
         compiler_params=pltpu.CompilerParams(
             collective_id=1, has_side_effects=True, vmem_limit_bytes=62 << 20
@@ -839,15 +919,43 @@
         cost_estimate=pl.CostEstimate(
             flops=26 * 10**9, bytes_accessed=100 * 10**6, transcendentals=0
         ),
-    )(out_rows, gate_up, x_rows, g_rows, hidden, pre_grad, rank, share)
+    )(out_rows, gate_up, x_rows, g_rows, hidden, pre_act, down_weight, rank, share)
+
+
+def last(out, grad, down, own, far):
+    steps = 4
+
+    def cut(shape):
+        return pl.BlockSpec((shape[0] // steps, shape[1]), lambda n: (n, 0))
+
+    row, wide, tall = (TOK, WIDTH), (512, 2 * HID), (HID, 512)
+    outs = (row, row, wide, tall)
+    return pl.pallas_call(
+        last_kernel,
+        grid=(steps,),
+        out_shape=tuple(jax.ShapeDtypeStruct(shape, BF16) for shape in outs),
+        in_specs=[
+            cut(row),
+            cut(row),
+            cut(tall),
+            cut(wide),
+            pl.BlockSpec((2, wide[0] // steps, wide[1]), lambda n: (0, n, 0)),
+        ],
+        out_specs=tuple(cut(shape) for shape in outs),
+        cost_estimate=pl.CostEstimate(
+            flops=10**6, bytes_accessed=12 * 10**6, transcendentals=0
+        ),
+    )(out, grad, down, own, far)
 
 
 def per_device(tokens, cotangent, expert_ids, gate_fixed, gate_up, down_weight):
-    out_rows, x_rows, g_rows, hidden, pre_grad, rank, share = dispatch(
+    out_rows, x_rows, g_rows, hidden, pre_act, rank, share = dispatch(
         expert_ids.T, gate_fixed.T, tokens, cotangent, gate_up, down_weight
     )
-    layer_out, token_grad, grad_in, grad_out = give_back(
-        out_rows, gate_up, x_rows, g_rows, hidden, pre_grad, rank, share
+    layer_out, token_grad, grad_in, grad_out = last(
+        *give_back(
+            out_rows, gate_up, x_rows, g_rows, hidden, pre_act, down_weight, rank, share
+        )
     )
     return layer_out, token_grad, grad_in[None], grad_out[None]
 

time: 190 us -> 184 us (0.968)
  local copies, waits for them, and re-layouts: 7.34 us -> 0 us
    unnamed x6 -> x0, local copies, waits for them, and re-layouts: 7.34 us -> none
    pallas_call x1, Pallas kernels: 85.7 us -> 79.4 us  [dispatch(): pl.pallas_call(dispatch_kernel, out_shape=(jax.ShapeDtypeStruct((ROWS, WI...]
    pallas_call x0 -> x1, Pallas kernels: none -> 5.18 us  [last(): pl.pallas_call(last_kernel, grid=(steps,), out_shape=tuple((jax.ShapeDtyp...]
    pallas_call x1, Pallas kernels: 95.1 us -> 97.7 us  [give_back(): pl.pallas_call(return_kernel, out_shape=(result, result, jax.ShapeDtypeSt...]
where the time goes in v3:
time: 184 us; the launch traced here: 183 us
  Pallas kernels  182 us (99%)
    pallas_call x1, Pallas kernels, give_back(): pl.pallas_call(return_kernel, out_shape=(result, result, jax.ShapeDtypeSt...  97.7 us
    pallas_call x1, Pallas kernels, dispatch(): pl.pallas_call(dispatch_kernel, out_shape=(jax.ShapeDtypeStruct((ROWS, WI...  79.4 us
    pallas_call x1, Pallas kernels, last(): pl.pallas_call(last_kernel, grid=(steps,), out_shape=tuple((jax.ShapeDtyp...  5.18 us

profile of v3, /device:TPU:0, one launch (start us, length us, event | category | flops | bytes accessed | tf_op | source)
XLA Modules:
  0.0 183.0 jit_solution(824934733659100994)
XLA Ops:
  0.6 79.4 %shard_map.93 = (bf16[528,4096]{1,0:T(8,128)(2,1)}, bf16[1056,2048]{1,0:T(8,128)(2,1)}, bf16[528,4096]{1,0:T(8,128)(2,1)}, bf16[1056,768]{1,0:T(8,128)(2,1)}, f3...) custom-call(s32[8,64]{1,0:T(8,128)} %bitcast.6, s32[8,64]{1,0:T(8,128)} %bitcast.7, ...), custom_call_target="tpu_custom_call" | custom-call | flops 20000000000 | bytes 40000000 | tf_op jit(solution)/shard_map/pallas_call | solution.py:821
  80.0 97.7 %shard_map.94 = (bf16[64,4096]{1,0:T(8,128)(2,1)}, bf16[64,4096]{1,0:T(8,128)(2,1)}, bf16[768,512]{1,0:T(8,128)(2,1)}, bf16[512,1536]{1,0:T(8,128)(2,1)}, bf16[2,512,1536]{2,1,0:T(8,128)(2,1)}) custom-call(bf16[528,4096]{1,0:T(8,128)(2,1)} %get-tuple-element.20.out_hbm, bf16[1,4096,1536]{2,1,0:T(8,128)(2,1)} %wgu_hbm.3, ...), custom_call_target="tpu_custom_call" | custom-call | flops 25999998976 | bytes 100000000 | tf_op jit(solution)/shard_map/pallas_call | solution.py:872
  177.8 5.2 %shard_map.95 = (bf16[64,4096]{1,0:T(8,128)(2,1)}, bf16[64,4096]{1,0:T(8,128)(2,1)}, bf16[512,1536]{1,0:T(8,128)(2,1)}, bf16[768,512]{1,0:T(8,128)(2,1)}) custom-call(bf16[64,4096]{1,0:T(8,128)(2,1)} %get-tuple-element.27.out_in, bf16[64,4096]{1,0:T(8,128)(2,1)} %get-tuple-element.28.grad_in, bf16[768,512]{1,0:T(8,128)(2,1)} %get-tuple-element.29.down_in, ...), custom_call_target="tpu_custom_call" | custom-call | flops 1000000 | bytes 12000000 | tf_op jit(solution)/shard_map/pallas_call | solution.py:933

commit v4 on v3

--- a/solution.py
+++ b/solution.py
@@ -435,8 +435,7 @@
     layer_out,
     token_grad,
     grad_out,
-    own_in,
-    far_in,
+    grad_in,
     xb,
     gb,
     gall,
@@ -449,6 +448,7 @@
     sum_out,
     near_in,
     near_out,
+    far_in,
     far_out,
     tail,
     compact,
@@ -492,10 +492,6 @@
     load("h", h_hbm, hb)
     for ahead in (2, 1, 3, 0):
         load(ahead, g_hbm.at[:, columns_of(ahead, core)], gb.at[mine, place_of(ahead)])
-    load("g", g_hbm, gall)
-    load("d", wd_hbm.at[0], wd)
-    load("pre", pre_hbm, pre)
-    load("x", x_hbm, xb)
     load_tail = pltpu.make_async_copy(
         out_hbm.at[pl.ds(16 * MAIN, 16), :], tail, local_sem.at[0]
     )
@@ -599,7 +595,6 @@
         return arrivals, owns
 
     def combine(which, arrivals, owns):
-        finals = []
         for route in range(2):
             for copy in arrivals[route]:
                 copy.wait_recv()
@@ -628,8 +623,12 @@
                     rest, rows_over[which, route], along, preferred_element_type=F32
                 )
                 partial[which, route, :, columns] = total.astype(BF16)
-            here = coord(first_axis(route))
-            for d in ORDER:
+
+    def pass_partial(which):
+        finals = []
+        for d in ORDER:
+            for route in range(2):
+                here = coord(first_axis(route))
                 there = lax.rem(here + d, 4)
                 copy = remote(
                     partial.at[which, route, pl.ds(pl.multiple_of(there * TOK, TOK), TOK), :],
@@ -717,17 +716,22 @@
             )
         return found
 
-    ends_out, ends_in = [], []
+    out_state = first_hop(0)
+    ends = []
     fetch["h"].wait()
     for ahead in (2, 1, 3):
         fetch[ahead].wait()
         swaps[ahead].wait_recv()
+        if ahead == 2:
+            load("g", g_hbm, gall)
+            load("d", wd_hbm.at[0], wd)
+            load("pre", pre_hbm, pre)
+            load("x", x_hbm, xb)
         weight_out(ahead)
         if ahead == 2:
             near_sent_out = pass_near(0)
-            out_state = first_hop(0)
         else:
-            ends_out.append(pass_far(0, ahead // 2))
+            ends.append(pass_far(0, ahead // 2))
     fetch["g"].wait()
     fetch["d"].wait()
     fetch["pre"].wait()
@@ -750,40 +754,46 @@
         pgb.at[mine], pgb.at[theirs], core_send.at[4], core_recv.at[4], other_core()
     )
     swap.start()
+    def token_side(first, end):
+        @pl.loop(first, end)
+        def _(n):
+            @pl.when(n + 1 < WIDTH // 256)
+            def _():
+                wgu_tile(n + 1).start()
+
+            wgu_tile(n).wait()
+            cols = pl.ds(pl.multiple_of(n * 256, 256), 256)
+            sig[:, cols] = lax.dot_general(
+                pgb[:ROWS, :],
+                wgu[lax.rem(n, 2)],
+                (((1,), (1,)), ((), ())),
+                preferred_element_type=F32,
+            ).astype(BF16)
+
+    token_side(0, 6)
     fetch["x"].wait()
     swap.wait_recv()
     weight_in(2)
     near_sent_in = pass_near(1)
-    ends_out += pass_sum(0, near_sent_out)
-    for ahead in (1, 3):
-        weight_in(ahead)
-        ends_in.append(pass_far(1, ahead // 2))
-
-    @pl.loop(0, WIDTH // 256)
-    def _(n):
-        @pl.when(n + 1 < WIDTH // 256)
-        def _():
-            wgu_tile(n + 1).start()
-
-        wgu_tile(n).wait()
-        cols = pl.ds(pl.multiple_of(n * 256, 256), 256)
-        sig[:, cols] = lax.dot_general(
-            pgb[:ROWS, :],
-            wgu[lax.rem(n, 2)],
-            (((1,), (1,)), ((), ())),
-            preferred_element_type=F32,
-        ).astype(BF16)
-
+    token_side(6, WIDTH // 256)
     sig_state = first_hop(1)
+    ends += pass_sum(0, near_sent_out)
     fetch[0].wait()
     swaps[0].wait_recv()
     weight_out(0)
     weight_in(0)
-    store_own = pltpu.make_async_copy(sum_in.at[0], own_in, local_sem.at[1])
-    store_own.start()
-    out_finals = combine(0, *out_state)
-    ends_in += pass_sum(1, near_sent_in)
-    for copy in ends_out:
+    combine(0, *out_state)
+    for ahead in (1, 3):
+        weight_in(ahead)
+        ends.append(pass_far(1, ahead // 2))
+    ends += pass_sum(1, near_sent_in)
+    for route in range(2):
+        for copy in sig_state[0][route]:
+            copy.wait_recv()
+    out_finals = pass_partial(0)
+    combine(1, [[], []], sig_state[1])
+    sig_finals = pass_partial(1)
+    for copy in ends[:4]:
         copy.wait_recv()
 
     @pl.loop(0, 4)
@@ -794,21 +804,28 @@
         grad_out[part, :] = total.astype(BF16)
 
     finish(0, out_finals, layer_out)
-    sig_finals = combine(1, *sig_state)
     finish(1, sig_finals, token_grad)
-    store_own.wait()
-    for copy in ends_in:
+    for copy in ends[4:]:
         copy.wait_recv()
+
+    @pl.loop(0, 4)
+    def _(n):
+        part = pl.ds(pl.multiple_of(n * 128, 128), 128)
+        total = sum_in[0, part, :].astype(F32)
+        total += far_in[0, part, :].astype(F32) + far_in[1, part, :].astype(F32)
+        sum_in[0, part, :] = total.astype(BF16)
+
+    store_in = pltpu.make_async_copy(sum_in.at[0], grad_in, local_sem.at[1])
+    store_in.start()
     for copy in sends + [swaps[ahead] for ahead in range(4)] + [swap]:
         copy.wait_send()
-
-
-def last_kernel(out_in, grad_in, down_in, own_in, far_in, layer_out, token_grad, gate_up, down):
-    layer_out[...] = out_in[...]
-    token_grad[...] = grad_in[...]
-    down[...] = down_in[...]
-    total = far_in[0].astype(F32) + far_in[1].astype(F32)
-    gate_up[...] = (total + own_in[...].astype(F32)).astype(BF16)
+    store_in.wait()
+
+
+def last_kernel(*refs):
+    count = len(refs) // 2
+    for src, dst in zip(refs[:count], refs[count:]):
+        dst[...] = src[...]
 
 
 VMEM = pl.BlockSpec(memory_space=pltpu.VMEM)
@@ -876,10 +893,9 @@
             result,
             jax.ShapeDtypeStruct((HID, 512), BF16),
             jax.ShapeDtypeStruct((512, 2 * HID), BF16),
-            jax.ShapeDtypeStruct((2, 512, 2 * HID), BF16),
         ),
         in_specs=[ANY] * 7 + [VMEM] * 2,
-        out_specs=(VMEM,) * 3 + (ANY,) * 2,
+        out_specs=(VMEM,) * 3 + (ANY,),
         scratch_shapes=[
             pltpu.VMEM((2 * ROWS, HALF), BF16),
             pltpu.VMEM((2 * ROWS, HALF), BF16),
@@ -893,6 +909,7 @@
             pltpu.VMEM((4, HID, 512), BF16),
             pltpu.VMEM((2, 256, 2 * HID), BF16),
             pltpu.VMEM((2, HID // 2, 512), BF16),
+            pltpu.VMEM((2, 512, 2 * HID), BF16),
             pltpu.VMEM((2, HID, 512), BF16),
             pltpu.VMEM((16, WIDTH), BF16),
             pltpu.VMEM((2, 2, 64, CHUNK), BF16),
@@ -922,37 +939,28 @@
     )(out_rows, gate_up, x_rows, g_rows, hidden, pre_act, down_weight, rank, share)
 
 
-def last(out, grad, down, own, far):
+def last(*results):
     steps = 4
-
-    def cut(shape):
-        return pl.BlockSpec((shape[0] // steps, shape[1]), lambda n: (n, 0))
-
-    row, wide, tall = (TOK, WIDTH), (512, 2 * HID), (HID, 512)
-    outs = (row, row, wide, tall)
+    specs = [
+        pl.BlockSpec((a.shape[0] // steps, a.shape[1]), lambda n: (n, 0)) for a in results
+    ]
     return pl.pallas_call(
         last_kernel,
         grid=(steps,),
-        out_shape=tuple(jax.ShapeDtypeStruct(shape, BF16) for shape in outs),
-        in_specs=[
-            cut(row),
-            cut(row),
-            cut(tall),
-            cut(wide),
-            pl.BlockSpec((2, wide[0] // steps, wide[1]), lambda n: (0, n, 0)),
-        ],
-        out_specs=tuple(cut(shape) for shape in outs),
+        out_shape=tuple(jax.ShapeDtypeStruct(a.shape, a.dtype) for a in results),
+        in_specs=specs,
+        out_specs=tuple(specs),
         cost_estimate=pl.CostEstimate(
-            flops=10**6, bytes_accessed=12 * 10**6, transcendentals=0
+            flops=0, bytes_accessed=7 * 10**6, transcendentals=0
         ),
-    )(out, grad, down, own, far)
+    )(*results)
 
 
 def per_device(tokens, cotangent, expert_ids, gate_fixed, gate_up, down_weight):
     out_rows, x_rows, g_rows, hidden, pre_act, rank, share = dispatch(
         expert_ids.T, gate_fixed.T, tokens, cotangent, gate_up, down_weight
     )
-    layer_out, token_grad, grad_in, grad_out = last(
+    layer_out, token_grad, grad_out, grad_in = last(
         *give_back(
             out_rows, gate_up, x_rows, g_rows, hidden, pre_act, down_weight, rank, share
         )

time: 184 us -> 176 us (0.957)
  Pallas kernels: 182 us -> 174 us
    pallas_call x1, Pallas kernels: 97.7 us -> 90.6 us  [give_back(): pl.pallas_call(return_kernel, out_shape=(result, result, jax.ShapeDtypeSt...]
where the time goes in v4:
time: 176 us; the launch traced here: 175 us
  Pallas kernels  174 us (99%)
    pallas_call x1, Pallas kernels, give_back(): pl.pallas_call(return_kernel, out_shape=(result, result, jax.ShapeDtypeSt...  90.6 us
    pallas_call x1, Pallas kernels, dispatch(): pl.pallas_call(dispatch_kernel, out_shape=(jax.ShapeDtypeStruct((ROWS, WI...  79.4 us
    pallas_call x1, Pallas kernels, last(): pl.pallas_call(last_kernel, grid=(steps,), out_shape=tuple((jax.ShapeDtyp...  4.34 us

profile of v4, /device:TPU:0, one launch (start us, length us, event | category | flops | bytes accessed | tf_op | source)
XLA Modules:
  0.0 175.0 jit_solution(12423974539868809007)
XLA Ops:
  0.6 79.4 %shard_map.93 = (bf16[528,4096]{1,0:T(8,128)(2,1)}, bf16[1056,2048]{1,0:T(8,128)(2,1)}, bf16[528,4096]{1,0:T(8,128)(2,1)}, bf16[1056,768]{1,0:T(8,128)(2,1)}, f3...) custom-call(s32[8,64]{1,0:T(8,128)} %bitcast.6, s32[8,64]{1,0:T(8,128)} %bitcast.7, ...), custom_call_target="tpu_custom_call" | custom-call | flops 20000000000 | bytes 40000000 | tf_op jit(solution)/shard_map/pallas_call | solution.py:838
  80.0 90.6 %shard_map.94 = (bf16[64,4096]{1,0:T(8,128)(2,1)}, bf16[64,4096]{1,0:T(8,128)(2,1)}, bf16[768,512]{1,0:T(8,128)(2,1)}, bf16[512,1536]{1,0:T(8,128)(2,1)}) custom-call(bf16[528,4096]{1,0:T(8,128)(2,1)} %get-tuple-element.19.out_hbm, bf16[1,4096,1536]{2,1,0:T(8,128)(2,1)} %wgu_hbm.3, bf16[1056,2048]{1,0:T(8,128)(2,1)} %get-tuple-element.20.x_hbm, ...), custom_call_target="tpu_custom_call" | custom-call | flops 25999998976 | bytes 100000000 | tf_op jit(solution)/shard_map/pallas_call | solution.py:889
  170.7 4.3 %shard_map.95 = (bf16[64,4096]{1,0:T(8,128)(2,1)}, bf16[64,4096]{1,0:T(8,128)(2,1)}, bf16[768,512]{1,0:T(8,128)(2,1)}, bf16[512,1536]{1,0:T(8,128)(2,1)}) custom-call(bf16[64,4096]{1,0:T(8,128)(2,1)} %get-tuple-element.26.refs_0_, bf16[64,4096]{1,0:T(8,128)(2,1)} %get-tuple-element.27.refs_1_, bf16[768,512]{1,0:T(8,128)(2,1)} %get-tuple-element.28.refs_2_, ...), custom_call_target="tpu_custom_call" | custom-call | bytes 7000000 | tf_op jit(solution)/shard_map/pallas_call | solution.py:947

commit v5 on v4

--- a/solution.py
+++ b/solution.py
@@ -149,40 +149,9 @@
     load_gu.start()
     load_d.start()
 
-    gates = gate_ref[...].astype(F32)
-    share = gates / jnp.sum(gates, axis=0, keepdims=True)
-    ids = ids_ref[...]
-    expert = iota((16, TOK), 0)
-    named = jnp.zeros((16, TOK), F32)
-    weight = jnp.zeros((16, TOK), F32)
-    for k in range(8):
-        hit = ids[k : k + 1, :] == expert
-        named += jnp.where(hit, 1.0, 0.0)
-        weight += jnp.where(hit, share[k : k + 1, :], 0.0)
-    before = jnp.where(iota((TOK, TOK), 0) < iota((TOK, TOK), 1), 1.0, 0.0)
-    rank = jnp.dot(named.astype(BF16), before.astype(BF16), preferred_element_type=F32)
-    rank = jnp.where(named > 0.0, rank, -1.0)
-    meta_own[...] = jnp.concatenate([rank, weight], axis=1)
-
     enter([peer(axis, d) for axis in ("z", "x") for d in ORDER] + [other_core()])
 
     sends = []
-    meta_recvs = []
-    for route in range(2):
-        here = coord(first_axis(route))
-        for d in ORDER:
-            copy = remote(
-                meta_own,
-                meta.at[route, here],
-                meta_send.at[route, d],
-                meta_recv.at[route, d],
-                peer(first_axis(route), d),
-            )
-            copy.start()
-            sends.append(copy)
-            meta_recvs.append(copy)
-        meta[route, pl.ds(here, 1)] = meta_own[...][None]
-
     sources = (tok_ref, cot_ref)
 
     def block(which, route, position, columns):
@@ -232,6 +201,38 @@
         return passed
 
     tok_copies = gather_start(0)
+
+    gates = gate_ref[...].astype(F32)
+    share = gates / jnp.sum(gates, axis=0, keepdims=True)
+    ids = ids_ref[...]
+    expert = iota((16, TOK), 0)
+    named = jnp.zeros((16, TOK), F32)
+    weight = jnp.zeros((16, TOK), F32)
+    for k in range(8):
+        hit = ids[k : k + 1, :] == expert
+        named += jnp.where(hit, 1.0, 0.0)
+        weight += jnp.where(hit, share[k : k + 1, :], 0.0)
+    before = jnp.where(iota((TOK, TOK), 0) < iota((TOK, TOK), 1), 1.0, 0.0)
+    rank = jnp.dot(named.astype(BF16), before.astype(BF16), preferred_element_type=F32)
+    rank = jnp.where(named > 0.0, rank, -1.0)
+    meta_own[...] = jnp.concatenate([rank, weight], axis=1)
+
+    meta_recvs = []
+    for route in range(2):
+        here = coord(first_axis(route))
+        for d in ORDER:
+            copy = remote(
+                meta_own,
+                meta.at[route, here],
+                meta_send.at[route, d],
+                meta_recv.at[route, d],
+                peer(first_axis(route), d),
+            )
+            copy.start()
+            sends.append(copy)
+            meta_recvs.append(copy)
+        meta[route, pl.ds(here, 1)] = meta_own[...][None]
+
     cot_copies = gather_start(1)
     for copy in meta_recvs:
         copy.wait_recv()
@@ -432,10 +433,13 @@
     wd_hbm,
     rank_ref,
     share_ref,
+    layer_hbm,
+    token_hbm,
+    down_hbm,
+    grad_in,
     layer_out,
     token_grad,
     grad_out,
-    grad_in,
     xb,
     gb,
     gall,
@@ -803,8 +807,18 @@
         total += far_out[0, part, :].astype(F32) + far_out[1, part, :].astype(F32)
         grad_out[part, :] = total.astype(BF16)
 
+    results = []
+
+    def leave(src, dst):
+        copy = pltpu.make_async_copy(src, dst, local_sem.at[27 + len(results)])
+        copy.start()
+        results.append(copy)
+
+    leave(grad_out, down_hbm)
     finish(0, out_finals, layer_out)
+    leave(layer_out, layer_hbm)
     finish(1, sig_finals, token_grad)
+    leave(token_grad, token_hbm)
     for copy in ends[4:]:
         copy.wait_recv()
 
@@ -819,13 +833,34 @@
     store_in.start()
     for copy in sends + [swaps[ahead] for ahead in range(4)] + [swap]:
         copy.wait_send()
-    store_in.wait()
+    for copy in results + [store_in]:
+        copy.wait()
 
 
 def last_kernel(*refs):
-    count = len(refs) // 2
-    for src, dst in zip(refs[:count], refs[count:]):
-        dst[...] = src[...]
+    count = len(refs) // 3
+    held, sems = refs[2 * count : 3 * count], refs[-1]
+    steps = 4
+    loads, stores = [], []
+    for n in range(count):
+        size = refs[n].shape[0] // steps
+        for step in range(steps):
+            part = pl.ds(step * size, size)
+            loads.append(
+                pltpu.make_async_copy(refs[n].at[part], held[n].at[part], sems.at[0, n, step])
+            )
+            stores.append(
+                pltpu.make_async_copy(
+                    held[n].at[part], refs[count + n].at[part], sems.at[1, n, step]
+                )
+            )
+    for copy in loads:
+        copy.start()
+    for load, store in zip(loads, stores):
+        load.wait()
+        store.start()
+    for copy in stores:
+        copy.wait()
 
 
 VMEM = pl.BlockSpec(memory_space=pltpu.VMEM)
@@ -895,8 +930,11 @@
             jax.ShapeDtypeStruct((512, 2 * HID), BF16),
         ),
         in_specs=[ANY] * 7 + [VMEM] * 2,
-        out_specs=(VMEM,) * 3 + (ANY,),
+        out_specs=(ANY,) * 4,
         scratch_shapes=[
+            pltpu.VMEM((TOK, WIDTH), BF16),
+            pltpu.VMEM((TOK, WIDTH), BF16),
+            pltpu.VMEM((HID, 512), BF16),
             pltpu.VMEM((2 * ROWS, HALF), BF16),
             pltpu.VMEM((2 * ROWS, HALF), BF16),
             pltpu.VMEM((ROWS, WIDTH), BF16),
@@ -917,7 +955,7 @@
             pltpu.VMEM((2, 2, 64, CHUNK), BF16),
             pltpu.VMEM((2, 2, 4 * TOK, HALF), BF16),
             pltpu.VMEM((2, 2, 3, TOK, HALF), BF16),
-            DMA((27,)),
+            DMA((30,)),
             DMA((2,)),
             DMA((2, 2, 4, 4)),
             DMA((2, 2, 4, 4)),
@@ -940,16 +978,13 @@
 
 
 def last(*results):
-    steps = 4
-    specs = [
-        pl.BlockSpec((a.shape[0] // steps, a.shape[1]), lambda n: (n, 0)) for a in results
-    ]
     return pl.pallas_call(
         last_kernel,
-        grid=(steps,),
         out_shape=tuple(jax.ShapeDtypeStruct(a.shape, a.dtype) for a in results),
-        in_specs=specs,
-        out_specs=tuple(specs),
+        in_specs=[ANY] * len(results),
+        out_specs=(ANY,) * len(results),
+        scratch_shapes=[pltpu.VMEM(a.shape, a.dtype) for a in results]
+        + [DMA((2, len(results), 4))],
         cost_estimate=pl.CostEstimate(
             flops=0, bytes_accessed=7 * 10**6, transcendentals=0
         ),

time: 176 us -> 175 us (level)
  Pallas kernels: 174 us -> 172 us
where the time goes in v5:
time: 175 us; the launch traced here: 173 us
  Pallas kernels  172 us (98%)
    pallas_call x1, Pallas kernels, give_back(): pl.pallas_call(return_kernel, out_shape=(result, result, jax.ShapeDtypeSt...  89.5 us
    pallas_call x1, Pallas kernels, dispatch(): pl.pallas_call(dispatch_kernel, out_shape=(jax.ShapeDtypeStruct((ROWS, WI...  79.4 us
    pallas_call x1, Pallas kernels, last(): pl.pallas_call(last_kernel, out_shape=tuple((jax.ShapeDtypeStruct(a.shape...  3.54 us

profile of v5, /device:TPU:0, one launch (start us, length us, event | category | flops | bytes accessed | tf_op | source)
XLA Modules:
  0.0 173.3 jit_solution(9879933697365402769)
XLA Ops:
  0.6 79.4 %shard_map.93 = (bf16[528,4096]{1,0:T(8,128)(2,1)}, bf16[1056,2048]{1,0:T(8,128)(2,1)}, bf16[528,4096]{1,0:T(8,128)(2,1)}, bf16[1056,768]{1,0:T(8,128)(2,1)}, f3...) custom-call(s32[8,64]{1,0:T(8,128)} %bitcast.6, s32[8,64]{1,0:T(8,128)} %bitcast.7, ...), custom_call_target="tpu_custom_call" | custom-call | flops 20000000000 | bytes 40000000 | tf_op jit(solution)/shard_map/pallas_call | solution.py:873
  80.1 89.5 %shard_map.94 = (bf16[64,4096]{1,0:T(8,128)(2,1)}, bf16[64,4096]{1,0:T(8,128)(2,1)}, bf16[768,512]{1,0:T(8,128)(2,1)}, bf16[512,1536]{1,0:T(8,128)(2,1)}) custom-call(bf16[528,4096]{1,0:T(8,128)(2,1)} %get-tuple-element.19.out_hbm, bf16[1,4096,1536]{2,1,0:T(8,128)(2,1)} %wgu_hbm.3, bf16[1056,2048]{1,0:T(8,128)(2,1)} %get-tuple-element.20.x_hbm, ...), custom_call_target="tpu_custom_call" | custom-call | flops 25999998976 | bytes 100000000 | tf_op jit(solution)/shard_map/pallas_call | solution.py:924
  169.6 3.5 %shard_map.95 = (bf16[64,4096]{1,0:T(8,128)(2,1)}, bf16[64,4096]{1,0:T(8,128)(2,1)}, bf16[768,512]{1,0:T(8,128)(2,1)}, bf16[512,1536]{1,0:T(8,128)(2,1)}) custom-call(bf16[64,4096]{1,0:T(8,128)(2,1)} %get-tuple-element.26.refs_0_, bf16[64,4096]{1,0:T(8,128)(2,1)} %get-tuple-element.27.refs_1_, bf16[768,512]{1,0:T(8,128)(2,1)} %get-tuple-element.28.refs_2_, ...), custom_call_target="tpu_custom_call" | custom-call | bytes 7000000 | tf_op jit(solution)/shard_map/pallas_call | solution.py:981

commit v6 on v5

--- a/solution.py
+++ b/solution.py
@@ -115,6 +115,7 @@
     g_hbm,
     h_hbm,
     pre_hbm,
+    far_hbm,
     rank_out,
     share_out,
     wgu,
@@ -131,6 +132,8 @@
     pre,
     hid,
     obuf,
+    far_rows,
+    far_sum,
     local_sem,
     meta_send,
     meta_recv,
@@ -241,6 +244,15 @@
         share_out[route] = jnp.concatenate([meta[route, s][:, TOK:] for s in range(4)], axis=1)
 
     buffers = (xbuf, g_hbm)
+    postponed = []
+    y = lax.axis_index("dp") // 2
+
+    def halves_of(route):
+        here = lax.rem(y, 2)
+        far = (1 - y // 2) == route
+        first = jnp.where(far, here, 1 - here)
+        return first, 1 - first
+
 
     def select(which, route, d):
         position = lax.rem(coord(second_axis(route)) + d, 4)
@@ -280,31 +292,9 @@
             return []
         staged_over[which, route, d - 1] = total.astype(BF16)
         device = peer(second_axis(route), d)
-        columns = pl.ds(route * HALF, HALF)
-        copies = []
-        if route == 0:
-            copies.append(
-                remote(
-                    staged.at[which, route, d - 1],
-                    target.at[pl.ds(pl.multiple_of(here * 128, 128), 128), columns],
-                    main_send.at[which, route, d, 0],
-                    main_recv.at[which, route, d, 0],
-                    device,
-                )
-            )
-        else:
-            for s in range(4):
-                first = pl.multiple_of((s * 4 + here) * MAIN, MAIN)
-                copies.append(
-                    remote(
-                        staged.at[which, route, d - 1, pl.ds(s * MAIN, MAIN), :],
-                        target.at[pl.ds(first, MAIN), columns],
-                        main_send.at[which, route, d, s],
-                        main_recv.at[which, route, d, s],
-                        device,
-                    )
-                )
-        copies.append(
+        size = HALF if which == 0 else HALF // 2
+        later = []
+        copies = [
             remote(
                 staged_over.at[which, route, d - 1],
                 over.at[which, route, mine, :],
@@ -312,10 +302,38 @@
                 over_recv.at[which, route, d],
                 device,
             )
-        )
+        ]
+        for part in range(HALF // size):
+            begin = 0 if which == 0 else pl.multiple_of(halves_of(route)[part] * size, size)
+            taken = pl.ds(begin, size)
+            columns = pl.ds(pl.multiple_of(route * HALF + begin, size), size)
+            found = later if part else copies
+            if route == 0:
+                found.append(
+                    remote(
+                        staged.at[which, route, d - 1, :, taken],
+                        target.at[pl.ds(pl.multiple_of(here * 128, 128), 128), columns],
+                        main_send.at[which, route, d, 4 * part],
+                        main_recv.at[which, route, d, 4 * part],
+                        device,
+                    )
+                )
+            else:
+                for s in range(4):
+                    first = pl.multiple_of((s * 4 + here) * MAIN, MAIN)
+                    found.append(
+                        remote(
+                            staged.at[which, route, d - 1, pl.ds(s * MAIN, MAIN), taken],
+                            target.at[pl.ds(first, MAIN), columns],
+                            main_send.at[which, route, d, 4 * part + s],
+                            main_recv.at[which, route, d, 4 * part + s],
+                            device,
+                        )
+                    )
         for copy in copies:
             copy.start()
         sends.extend(copies)
+        postponed.extend(later)
         return copies
 
     def second_hop(which, passed):
@@ -347,6 +365,9 @@
     cot_passed = gather_pass(1, cot_copies)
     x_arrivals = second_hop(0, tok_passed)
     g_arrivals = second_hop(1, cot_passed)
+    for copy in postponed:
+        copy.start()
+    sends.extend(postponed)
     for which in range(2):
         for route in range(2):
             select(which, route, 0)
@@ -361,13 +382,16 @@
         copy = pltpu.make_async_copy(src, dst, local_sem.at[2 + len(stores)])
         copy.start()
         stores.append(copy)
+        return copy
 
     def share(src, dst):
         slot = len(shared)
         copy = remote(src, dst, core_send.at[slot], core_recv.at[slot], other_core())
         copy.start()
         shared.append(copy)
-
+        return copy
+
+    before_own = len(stores)
     for route in range(2):
         here = coord(second_axis(route))
         columns = pl.ds(route * HALF, HALF)
@@ -382,6 +406,7 @@
                     g_hbm.at[pl.ds(first, MAIN), columns],
                 )
 
+    own_stores = stores[before_own:]
     mine, theirs = pl.ds(0, ROWS), pl.ds(ROWS, ROWS)
 
     def split(src, dst):
@@ -403,22 +428,55 @@
         pre[:, u_cols] = u
         v = jnp.dot(xbuf[...], wgu[:, v_cols], preferred_element_type=F32)
         pre[:, v_cols] = v
-        hid[:, u_cols] = (pre[:, u_cols] * jax.nn.sigmoid(pre[:, u_cols]) * v).astype(BF16)
-
-    share(hid, h_hbm.at[theirs])
+        hid[:ROWS, u_cols] = (pre[:, u_cols] * jax.nn.sigmoid(pre[:, u_cols]) * v).astype(BF16)
+
+    hid_share = share(hid.at[mine], hid.at[theirs])
     store(pre, pre_hbm)
-    store(hid, h_hbm.at[mine])
-
-    @pl.loop(0, WIDTH // 256)
+    finish(1, g_arrivals)
+    own_stores.append(store(own_over, g_hbm.at[pl.ds(16 * MAIN, 16), :]))
+    for copy in own_stores:
+        copy.wait()
+
+    def far_columns(of_core):
+        return pl.ds(pl.multiple_of((2 * lax.rem(y + 2, 4) + of_core) * 512, 512), 512)
+
+    far_load = store(g_hbm.at[:, far_columns(core)], far_rows.at[mine])
+    far_share = share(g_hbm.at[:, far_columns(1 - core)], far_rows.at[theirs])
+
+    @pl.loop(0, HALF // 256)
     def _(n):
         cols = pl.ds(pl.multiple_of(n * 256, 256), 256)
-        obuf[:, cols] = jnp.dot(hid[...], wd[:, cols], preferred_element_type=F32).astype(BF16)
+        obuf[:, cols] = jnp.dot(
+            hid[:ROWS, :], wd[:, cols], preferred_element_type=F32
+        ).astype(BF16)
 
     store(obuf, out_hbm)
-    finish(1, g_arrivals)
-    store(own_over, g_hbm.at[pl.ds(16 * MAIN, 16), :])
-    for copy in stores + shared:
-        copy.wait()
+    hid_share.wait_recv()
+    store(hid, h_hbm)
+    far_load.wait()
+    far_share.wait_recv()
+
+    @pl.loop(0, 3)
+    def _(n):
+        piece = pl.ds(pl.multiple_of(n * 256, 256), 256)
+        far_sum[piece, :] = lax.dot_general(
+            hid[:, piece],
+            far_rows[...],
+            (((0,), (0,)), ((), ())),
+            preferred_element_type=F32,
+        ).astype(BF16)
+
+    store(far_sum, far_hbm)
+    for copy in postponed:
+        copy.wait_recv()
+    for copy in stores:
+        if copy is not far_load and all(copy is not other for other in own_stores):
+            copy.wait()
+    for copy in shared:
+        if copy is hid_share or copy is far_share:
+            copy.wait_send()
+        else:
+            copy.wait()
     for copy in sends:
         copy.wait_send()
 
@@ -430,6 +488,7 @@
     g_hbm,
     h_hbm,
     pre_hbm,
+    far_hbm,
     wd_hbm,
     rank_ref,
     share_ref,
@@ -477,7 +536,6 @@
     y = lax.axis_index("dp") // 2
     core = lax.rem(lax.axis_index("dp"), 2)
     sig = gall
-    inputs = (out_hbm, sig)
     mine, theirs = pl.ds(0, ROWS), pl.ds(ROWS, ROWS)
     fetch = {}
 
@@ -494,10 +552,11 @@
         return pl.ds(pl.multiple_of(lax.rem(y + ahead, 4) * 512, 512), 512)
 
     load("h", h_hbm, hb)
-    for ahead in (2, 1, 3, 0):
+    load("d", wd_hbm.at[0], wd)
+    for ahead in (1, 3, 0):
         load(ahead, g_hbm.at[:, columns_of(ahead, core)], gb.at[mine, place_of(ahead)])
     load_tail = pltpu.make_async_copy(
-        out_hbm.at[pl.ds(16 * MAIN, 16), :], tail, local_sem.at[0]
+        out_hbm.at[pl.ds(16 * MAIN, 16), :], tail.at[:, pl.ds(0, HALF)], local_sem.at[0]
     )
     load_tail.start()
 
@@ -513,39 +572,32 @@
         + [other_core()]
     )
     sends = []
-    swaps = {}
-    for ahead in (2, 1, 3, 0):
-        swaps[ahead] = remote(
-            g_hbm.at[:, columns_of(ahead, 1 - core)],
-            gb.at[theirs, place_of(ahead)],
-            core_send.at[ahead],
-            core_recv.at[ahead],
-            other_core(),
-        )
-        swaps[ahead].start()
-
     def pieces(which, route, position, slot):
         columns = pl.ds(route * HALF, HALF)
         if route == 0:
-            first = pl.multiple_of(position * 128, 128)
-            return [
-                (inputs[which].at[pl.ds(first, 128), columns], rows.at[which, route, slot])
-            ]
+            rows_there = pl.ds(pl.multiple_of(position * 128, 128), 128)
+            if which == 0:
+                src = out_hbm.at[rows_there]
+            else:
+                src = sig.at[rows_there, columns]
+            return [(src, rows.at[which, route, slot])]
         found = []
         for s in range(4):
-            first = pl.multiple_of((s * 4 + position) * MAIN, MAIN)
-            found.append(
-                (
-                    inputs[which].at[pl.ds(first, MAIN), columns],
-                    rows.at[which, route, slot, pl.ds(s * MAIN, MAIN), :],
-                )
-            )
+            dst = rows.at[which, route, slot, pl.ds(s * MAIN, MAIN), :]
+            if which == 0:
+                first = pl.multiple_of((s % 2) * 128 + position * MAIN, MAIN)
+                found.append((partial.at[1, s // 2, pl.ds(first, MAIN), :], dst))
+            else:
+                first = pl.multiple_of((s * 4 + position) * MAIN, MAIN)
+                found.append((sig.at[pl.ds(first, MAIN), columns], dst))
         return found
 
-    def first_hop(which):
+    early = []
+
+    def first_hop(which, routes):
         arrivals = [[], []]
         for d in ORDER:
-            for route in range(2):
+            for route in routes:
                 here = coord(second_axis(route))
                 there = lax.rem(here + d, 4)
                 for s, (src, dst) in enumerate(pieces(which, route, there, here)):
@@ -557,19 +609,19 @@
                         peer(second_axis(route), d),
                     )
                     copy.start()
-                    sends.append(copy)
+                    (early if which == 0 and route == 1 else sends).append(copy)
                     arrivals[route].append(copy)
         owns = [[], []]
-        for route in range(2):
+        for route in routes:
             here = coord(second_axis(route))
             for s, (src, dst) in enumerate(pieces(which, route, here, here)):
                 copy = pltpu.make_async_copy(src, dst, local_sem.at[2 + which * 8 + route * 4 + s])
                 copy.start()
                 owns[route].append(copy)
-        if which == 0:
+        if which == 0 and routes[0] == 0:
             load_tail.wait()
         last = tail if which == 0 else sig.at[pl.ds(16 * MAIN, 16), :]
-        for route in range(2):
+        for route in routes:
             here = coord(second_axis(route))
             slot, chunk = overflow_target(route, (64, 16), 0)
             total = jnp.zeros((64, CHUNK), F32)
@@ -689,8 +741,11 @@
     halves = (half_out, half_in)
 
     def pass_half(kind, ahead, half, side, dst, slot):
+        src = far_hbm.at[halves[kind][half], :]
+        if kind or ahead != 2:
+            src = sums[kind].at[ahead, halves[kind][half], :]
         copy = remote(
-            sums[kind].at[ahead, halves[kind][half], :],
+            src,
             dst,
             dp_send.at[slot, side, kind],
             dp_recv.at[slot, side, kind],
@@ -720,24 +775,43 @@
             )
         return found
 
-    out_state = first_hop(0)
+    near_sent_out = pass_near(0)
+    swaps = {}
+    for ahead in (1, 3, 0):
+        swaps[ahead] = remote(
+            g_hbm.at[:, columns_of(ahead, 1 - core)],
+            gb.at[theirs, place_of(ahead)],
+            core_send.at[ahead],
+            core_recv.at[ahead],
+            other_core(),
+        )
+        swaps[ahead].start()
+
+    out_state = first_hop(0, (0,))
     ends = []
     fetch["h"].wait()
-    for ahead in (2, 1, 3):
+    fetch["d"].wait()
+    load("g", g_hbm, gall)
+    load("pre", pre_hbm, pre)
+    load("x", x_hbm, xb)
+
+    @pl.loop(0, HALF // 256)
+    def _(n):
+        cols = pl.ds(pl.multiple_of(n * 256, 256), 256)
+        there = pl.ds(pl.multiple_of(HALF + n * 256, 256), 256)
+        tile = jnp.dot(hb[:ROWS, :], wd[:, there], preferred_element_type=F32).astype(BF16)
+        partial[1, 0, :, cols] = tile[:256]
+        partial[1, 1, :, cols] = tile[256:512]
+        tail[:, there] = tile[512:]
+
+    for old, new in zip(out_state, first_hop(0, (1,))):
+        old[1] = new[1]
+    for ahead in (1, 3):
         fetch[ahead].wait()
         swaps[ahead].wait_recv()
-        if ahead == 2:
-            load("g", g_hbm, gall)
-            load("d", wd_hbm.at[0], wd)
-            load("pre", pre_hbm, pre)
-            load("x", x_hbm, xb)
         weight_out(ahead)
-        if ahead == 2:
-            near_sent_out = pass_near(0)
-        else:
-            ends.append(pass_far(0, ahead // 2))
+        ends.append(pass_far(0, ahead // 2))
     fetch["g"].wait()
-    fetch["d"].wait()
     fetch["pre"].wait()
 
     @pl.loop(0, 3)
@@ -780,7 +854,7 @@
     weight_in(2)
     near_sent_in = pass_near(1)
     token_side(6, WIDTH // 256)
-    sig_state = first_hop(1)
+    sig_state = first_hop(1, (0, 1))
     ends += pass_sum(0, near_sent_out)
     fetch[0].wait()
     swaps[0].wait_recv()
@@ -795,6 +869,8 @@
         for copy in sig_state[0][route]:
             copy.wait_recv()
     out_finals = pass_partial(0)
+    for copy in early:
+        copy.wait_send()
     combine(1, [[], []], sig_state[1])
     sig_finals = pass_partial(1)
     for copy in ends[:4]:
@@ -831,7 +907,7 @@
 
     store_in = pltpu.make_async_copy(sum_in.at[0], grad_in, local_sem.at[1])
     store_in.start()
-    for copy in sends + [swaps[ahead] for ahead in range(4)] + [swap]:
+    for copy in sends + [swaps[ahead] for ahead in (1, 3, 0)] + [swap]:
         copy.wait_send()
     for copy in results + [store_in]:
         copy.wait()
@@ -873,16 +949,17 @@
     return pl.pallas_call(
         dispatch_kernel,
         out_shape=(
-            jax.ShapeDtypeStruct((ROWS, WIDTH), BF16),
+            jax.ShapeDtypeStruct((ROWS, HALF), BF16),
             jax.ShapeDtypeStruct((2 * ROWS, HALF), BF16),
             jax.ShapeDtypeStruct((ROWS, WIDTH), BF16),
             jax.ShapeDtypeStruct((2 * ROWS, HID), BF16),
             jax.ShapeDtypeStruct((ROWS, 2 * HID), F32),
+            jax.ShapeDtypeStruct((HID, 512), BF16),
             table,
             table,
         ),
         in_specs=[VMEM] * 4 + [ANY] * 2,
-        out_specs=(ANY,) * 5 + (VMEM,) * 2,
+        out_specs=(ANY,) * 6 + (VMEM,) * 2,
         scratch_shapes=[
             pltpu.VMEM((WIDTH, 2 * HID), BF16),
             pltpu.VMEM((HID, WIDTH), BF16),
@@ -896,19 +973,21 @@
             pltpu.VMEM((2, 4 * MAIN, HALF), BF16),
             pltpu.VMEM((16, WIDTH), BF16),
             pltpu.VMEM((ROWS, 2 * HID), F32),
-            pltpu.VMEM((ROWS, HID), BF16),
-            pltpu.VMEM((ROWS, WIDTH), BF16),
-            DMA((16,)),
+            pltpu.VMEM((2 * ROWS, HID), BF16),
+            pltpu.VMEM((ROWS, HALF), BF16),
+            pltpu.VMEM((2 * ROWS, 512), BF16),
+            pltpu.VMEM((HID, 512), BF16),
+            DMA((20,)),
             DMA((2, 4)),
             DMA((2, 4)),
             DMA((2, 2, 4)),
             DMA((2, 2, 4)),
-            DMA((2, 2, 4, 4)),
-            DMA((2, 2, 4, 4)),
+            DMA((2, 2, 4, 8)),
+            DMA((2, 2, 4, 8)),
             DMA((2, 2, 4)),
             DMA((2, 2, 4)),
-            DMA((5,)),
-            DMA((5,)),
+            DMA((6,)),
+            DMA((6,)),
         ],
         compiler_params=pltpu.CompilerParams(
             collective_id=0, has_side_effects=True, vmem_limit_bytes=60 << 20
@@ -919,7 +998,7 @@
     )(ids, gates, tokens, cotangent, gate_up, down_weight)
 
 
-def give_back(out_rows, gate_up, x_rows, g_rows, hidden, pre_act, down_weight, rank, share):
+def give_back(out_rows, gate_up, x_rows, g_rows, hidden, pre_act, far_sum, down_weight, rank, share):
     result = jax.ShapeDtypeStruct((TOK, WIDTH), BF16)
     return pl.pallas_call(
         return_kernel,
@@ -929,7 +1008,7 @@
             jax.ShapeDtypeStruct((HID, 512), BF16),
             jax.ShapeDtypeStruct((512, 2 * HID), BF16),
         ),
-        in_specs=[ANY] * 7 + [VMEM] * 2,
+        in_specs=[ANY] * 8 + [VMEM] * 2,
         out_specs=(ANY,) * 4,
         scratch_shapes=[
             pltpu.VMEM((TOK, WIDTH), BF16),
@@ -974,7 +1053,7 @@
         cost_estimate=pl.CostEstimate(
             flops=26 * 10**9, bytes_accessed=100 * 10**6, transcendentals=0
         ),
-    )(out_rows, gate_up, x_rows, g_rows, hidden, pre_act, down_weight, rank, share)
+    )(out_rows, gate_up, x_rows, g_rows, hidden, pre_act, far_sum, down_weight, rank, share)
 
 
 def last(*results):
@@ -992,12 +1071,12 @@
 
 
 def per_device(tokens, cotangent, expert_ids, gate_fixed, gate_up, down_weight):
-    out_rows, x_rows, g_rows, hidden, pre_act, rank, share = dispatch(
+    out_rows, x_rows, g_rows, hidden, pre_act, far_sum, rank, share = dispatch(
         expert_ids.T, gate_fixed.T, tokens, cotangent, gate_up, down_weight
     )
     layer_out, token_grad, grad_out, grad_in = last(
         *give_back(
-            out_rows, gate_up, x_rows, g_rows, hidden, pre_act, down_weight, rank, share
+            out_rows, gate_up, x_rows, g_rows, hidden, pre_act, far_sum, down_weight, rank, share
         )
     )
     return layer_out, token_grad, grad_in[None], grad_out[None]

time: 175 us -> 172 us (0.983)
    pallas_call x1, Pallas kernels: 79.4 us -> 76.8 us  [dispatch(): pl.pallas_call(dispatch_kernel, out_shape=(jax.ShapeDtypeStruct((ROWS, HA...]
where the time goes in v6:
time: 172 us
  Pallas kernels  171 us (99%)
    pallas_call x1, Pallas kernels, give_back(): pl.pallas_call(return_kernel, out_shape=(result, result, jax.ShapeDtypeSt...  90.5 us
    pallas_call x1, Pallas kernels, dispatch(): pl.pallas_call(dispatch_kernel, out_shape=(jax.ShapeDtypeStruct((ROWS, HA...  76.8 us
    pallas_call x1, Pallas kernels, last(): pl.pallas_call(last_kernel, out_shape=tuple((jax.ShapeDtypeStruct(a.shape...  3.54 us

profile of v6, /device:TPU:0, one launch (start us, length us, event | category | flops | bytes accessed | tf_op | source)
XLA Modules:
  0.0 171.7 jit_solution(9836056753565316708)
XLA Ops:
  0.6 76.8 %shard_map.93 = (bf16[528,2048]{1,0:T(8,128)(2,1)}, bf16[1056,2048]{1,0:T(8,128)(2,1)}, bf16[528,4096]{1,0:T(8,128)(2,1)}, bf16[1056,768]{1,0:T(8,128)(2,1)}, f3...) custom-call(s32[8,64]{1,0:T(8,128)} %bitcast.6, ...), custom_call_target="tpu_custom_call" | custom-call | flops 20000000000 | bytes 40000000 | tf_op jit(solution)/shard_map/pallas_call | solution.py:949
  77.4 90.5 %shard_map.94 = (bf16[64,4096]{1,0:T(8,128)(2,1)}, bf16[64,4096]{1,0:T(8,128)(2,1)}, bf16[768,512]{1,0:T(8,128)(2,1)}, bf16[512,1536]{1,0:T(8,128)(2,1)}) custom-call(bf16[528,2048]{1,0:T(8,128)(2,1)} %get-tuple-element.20.out_hbm, bf16[1,4096,1536]{2,1,0:T(8,128)(2,1)} %wgu_hbm.3, bf16[1056,2048]{1,0:T(8,128)(2,1)} %get-tuple-element.21.x_hbm, ...), custom_call_target="tpu_custom_call" | custom-call | flops 25999998976 | bytes 100000000 | tf_op jit(solution)/shard_map/pallas_call | solution.py:1003
  168.0 3.5 %shard_map.95 = (bf16[64,4096]{1,0:T(8,128)(2,1)}, bf16[64,4096]{1,0:T(8,128)(2,1)}, bf16[768,512]{1,0:T(8,128)(2,1)}, bf16[512,1536]{1,0:T(8,128)(2,1)}) custom-call(bf16[64,4096]{1,0:T(8,128)(2,1)} %get-tuple-element.28.refs_0_, bf16[64,4096]{1,0:T(8,128)(2,1)} %get-tuple-element.29.refs_1_, bf16[768,512]{1,0:T(8,128)(2,1)} %get-tuple-element.30.refs_2_, ...), custom_call_target="tpu_custom_call" | custom-call | bytes 7000000 | tf_op jit(solution)/shard_map/pallas_call | solution.py:1060

commit v7 on v6

--- a/solution.py
+++ b/solution.py
@@ -832,6 +832,7 @@
         pgb.at[mine], pgb.at[theirs], core_send.at[4], core_recv.at[4], other_core()
     )
     swap.start()
+    ends += pass_sum(0, near_sent_out)
     def token_side(first, end):
         @pl.loop(first, end)
         def _(n):
@@ -855,12 +856,12 @@
     near_sent_in = pass_near(1)
     token_side(6, WIDTH // 256)
     sig_state = first_hop(1, (0, 1))
-    ends += pass_sum(0, near_sent_out)
     fetch[0].wait()
     swaps[0].wait_recv()
     weight_out(0)
     weight_in(0)
     combine(0, *out_state)
+    out_finals = pass_partial(0)
     for ahead in (1, 3):
         weight_in(ahead)
         ends.append(pass_far(1, ahead // 2))
@@ -868,7 +869,6 @@
     for route in range(2):
         for copy in sig_state[0][route]:
             copy.wait_recv()
-    out_finals = pass_partial(0)
     for copy in early:
         copy.wait_send()
     combine(1, [[], []], sig_state[1])
@@ -897,19 +897,16 @@
     leave(token_grad, token_hbm)
     for copy in ends[4:]:
         copy.wait_recv()
-
-    @pl.loop(0, 4)
-    def _(n):
-        part = pl.ds(pl.multiple_of(n * 128, 128), 128)
+    for n in range(4):
+        part = pl.ds(n * 128, 128)
         total = sum_in[0, part, :].astype(F32)
         total += far_in[0, part, :].astype(F32) + far_in[1, part, :].astype(F32)
         sum_in[0, part, :] = total.astype(BF16)
-
-    store_in = pltpu.make_async_copy(sum_in.at[0], grad_in, local_sem.at[1])
-    store_in.start()
+        leave(sum_in.at[0, part, :], grad_in.at[part, :])
+
     for copy in sends + [swaps[ahead] for ahead in (1, 3, 0)] + [swap]:
         copy.wait_send()
-    for copy in results + [store_in]:
+    for copy in results:
         copy.wait()
 
 
@@ -1034,7 +1031,7 @@
             pltpu.VMEM((2, 2, 64, CHUNK), BF16),
             pltpu.VMEM((2, 2, 4 * TOK, HALF), BF16),
             pltpu.VMEM((2, 2, 3, TOK, HALF), BF16),
-            DMA((30,)),
+            DMA((34,)),
             DMA((2,)),
             DMA((2, 2, 4, 4)),
             DMA((2, 2, 4, 4)),

time: 172 us -> 168 us (0.977)
  Pallas kernels: 171 us -> 166 us
    pallas_call x1, Pallas kernels: 90.5 us -> 85.7 us  [give_back(): pl.pallas_call(return_kernel, out_shape=(result, result, jax.ShapeDtypeSt...]
where the time goes in v7:
time: 168 us; the launch traced here: 167 us
  Pallas kernels  166 us (99%)
    pallas_call x1, Pallas kernels, give_back(): pl.pallas_call(return_kernel, out_shape=(result, result, jax.ShapeDtypeSt...  85.7 us
    pallas_call x1, Pallas kernels, dispatch(): pl.pallas_call(dispatch_kernel, out_shape=(jax.ShapeDtypeStruct((ROWS, HA...  76.8 us
    pallas_call x1, Pallas kernels, last(): pl.pallas_call(last_kernel, out_shape=tuple((jax.ShapeDtypeStruct(a.shape...  3.54 us

profile of v7, /device:TPU:0, one launch (start us, length us, event | category | flops | bytes accessed | tf_op | source)
XLA Modules:
  0.0 166.8 jit_solution(9034448322041589712)
XLA Ops:
  0.6 76.8 %shard_map.93 = (bf16[528,2048]{1,0:T(8,128)(2,1)}, bf16[1056,2048]{1,0:T(8,128)(2,1)}, bf16[528,4096]{1,0:T(8,128)(2,1)}, bf16[1056,768]{1,0:T(8,128)(2,1)}, f3...) custom-call(s32[8,64]{1,0:T(8,128)} %bitcast.6, ...), custom_call_target="tpu_custom_call" | custom-call | flops 20000000000 | bytes 40000000 | tf_op jit(solution)/shard_map/pallas_call | solution.py:946
  77.4 85.7 %shard_map.94 = (bf16[64,4096]{1,0:T(8,128)(2,1)}, bf16[64,4096]{1,0:T(8,128)(2,1)}, bf16[768,512]{1,0:T(8,128)(2,1)}, bf16[512,1536]{1,0:T(8,128)(2,1)}) custom-call(bf16[528,2048]{1,0:T(8,128)(2,1)} %get-tuple-element.20.out_hbm, bf16[1,4096,1536]{2,1,0:T(8,128)(2,1)} %wgu_hbm.3, bf16[1056,2048]{1,0:T(8,128)(2,1)} %get-tuple-element.21.x_hbm, ...), custom_call_target="tpu_custom_call" | custom-call | flops 25999998976 | bytes 100000000 | tf_op jit(solution)/shard_map/pallas_call | solution.py:1000
  163.1 3.5 %shard_map.95 = (bf16[64,4096]{1,0:T(8,128)(2,1)}, bf16[64,4096]{1,0:T(8,128)(2,1)}, bf16[768,512]{1,0:T(8,128)(2,1)}, bf16[512,1536]{1,0:T(8,128)(2,1)}) custom-call(bf16[64,4096]{1,0:T(8,128)(2,1)} %get-tuple-element.28.refs_0_, bf16[64,4096]{1,0:T(8,128)(2,1)} %get-tuple-element.29.refs_1_, bf16[768,512]{1,0:T(8,128)(2,1)} %get-tuple-element.30.refs_2_, ...), custom_call_target="tpu_custom_call" | custom-call | bytes 7000000 | tf_op jit(solution)/shard_map/pallas_call | solution.py:1057

commit v8 on v7

--- a/solution.py
+++ b/solution.py
@@ -766,13 +766,24 @@
         found = []
         for side, ahead in ((0, 1), (1, 3)):
             near[side].wait_recv()
-            part = halves[kind][side]
-            sums[kind][ahead, part, :] = (
-                sums[kind][ahead, part, :].astype(F32) + nears[kind][side].astype(F32)
-            ).astype(BF16)
-            found.append(
-                pass_half(kind, ahead, side, side, fars[kind].at[side, part, :], 2)
-            )
+            whole = halves[kind][side]
+            size = whole.size // (1 + kind)
+            for piece in range(1 + kind):
+                part = pl.ds(whole.start + piece * size, size)
+                arrived = nears[kind][side, piece * size : (piece + 1) * size, :]
+                sums[kind][ahead, part, :] = (
+                    sums[kind][ahead, part, :].astype(F32) + arrived.astype(F32)
+                ).astype(BF16)
+                copy = remote(
+                    sums[kind].at[ahead, part, :],
+                    fars[kind].at[side, part, :],
+                    dp_send.at[2 + piece, side, kind],
+                    dp_recv.at[2 + piece, side, kind],
+                    along_y((1, 3)[side]),
+                )
+                copy.start()
+                sends.append(copy)
+                found.append(copy)
         return found
 
     near_sent_out = pass_near(0)
@@ -895,9 +906,10 @@
     leave(layer_out, layer_hbm)
     finish(1, sig_finals, token_grad)
     leave(token_grad, token_hbm)
-    for copy in ends[4:]:
+    for copy in ends[4:6]:
         copy.wait_recv()
-    for n in range(4):
+    for n, copy in ((0, ends[6]), (2, ends[8]), (1, ends[7]), (3, ends[9])):
+        copy.wait_recv()
         part = pl.ds(n * 128, 128)
         total = sum_in[0, part, :].astype(F32)
         total += far_in[0, part, :].astype(F32) + far_in[1, part, :].astype(F32)
@@ -1039,8 +1051,8 @@
             DMA((2, 2, 4)),
             DMA((2, 2, 4)),
             DMA((2, 2, 4)),
-            DMA((3, 2, 2)),
-            DMA((3, 2, 2)),
+            DMA((4, 2, 2)),
+            DMA((4, 2, 2)),
             DMA((5,)),
             DMA((5,)),
         ],

time: 168 us -> 167 us (level)
  no operation moved by 1% of the time
where the time goes in v8:
time: 167 us
  Pallas kernels  166 us (99%)
    pallas_call x1, Pallas kernels, give_back(): pl.pallas_call(return_kernel, out_shape=(result, result, jax.ShapeDtypeSt...  85.5 us
    pallas_call x1, Pallas kernels, dispatch(): pl.pallas_call(dispatch_kernel, out_shape=(jax.ShapeDtypeStruct((ROWS, HA...  76.8 us
    pallas_call x1, Pallas kernels, last(): pl.pallas_call(last_kernel, out_shape=tuple((jax.ShapeDtypeStruct(a.shape...  3.54 us

profile of v8, /device:TPU:0, one launch (start us, length us, event | category | flops | bytes accessed | tf_op | source)
XLA Modules:
  0.0 166.6 jit_solution(3144022517895136020)
XLA Ops:
  0.6 76.8 %shard_map.93 = (bf16[528,2048]{1,0:T(8,128)(2,1)}, bf16[1056,2048]{1,0:T(8,128)(2,1)}, bf16[528,4096]{1,0:T(8,128)(2,1)}, bf16[1056,768]{1,0:T(8,128)(2,1)}, f3...) custom-call(s32[8,64]{1,0:T(8,128)} %bitcast.6, ...), custom_call_target="tpu_custom_call" | custom-call | flops 20000000000 | bytes 40000000 | tf_op jit(solution)/shard_map/pallas_call | solution.py:958
  77.4 85.5 %shard_map.94 = (bf16[64,4096]{1,0:T(8,128)(2,1)}, bf16[64,4096]{1,0:T(8,128)(2,1)}, bf16[768,512]{1,0:T(8,128)(2,1)}, bf16[512,1536]{1,0:T(8,128)(2,1)}) custom-call(bf16[528,2048]{1,0:T(8,128)(2,1)} %get-tuple-element.20.out_hbm, bf16[1,4096,1536]{2,1,0:T(8,128)(2,1)} %wgu_hbm.3, bf16[1056,2048]{1,0:T(8,128)(2,1)} %get-tuple-element.21.x_hbm, ...), custom_call_target="tpu_custom_call" | custom-call | flops 25999998976 | bytes 100000000 | tf_op jit(solution)/shard_map/pallas_call | solution.py:1012
  162.9 3.5 %shard_map.95 = (bf16[64,4096]{1,0:T(8,128)(2,1)}, bf16[64,4096]{1,0:T(8,128)(2,1)}, bf16[768,512]{1,0:T(8,128)(2,1)}, bf16[512,1536]{1,0:T(8,128)(2,1)}) custom-call(bf16[64,4096]{1,0:T(8,128)(2,1)} %get-tuple-element.28.refs_0_, bf16[64,4096]{1,0:T(8,128)(2,1)} %get-tuple-element.29.refs_1_, bf16[768,512]{1,0:T(8,128)(2,1)} %get-tuple-element.30.refs_2_, ...), custom_call_target="tpu_custom_call" | custom-call | bytes 7000000 | tf_op jit(solution)/shard_map/pallas_call | solution.py:1069
